TPU v7x, 32 devices: a whole 2x2x4 slice. The times are simulated.
32 devices in a mesh: gx: 4 (over x, core), gy: 8 (over z, y).
Axes of the slice: x: 2, y: 2, z: 4, core: 2. Of those that a mesh axis runs over, the one named last changes fastest.
Arguments:
- bond_mask: int32 [3, 64, 128, 128], P(None, 'gx', 'gy'), may hold values 0 or 1
- levels: float32 [2, 3], replicated, may hold values from 0.3 to 3
- electrode: int32 [2, 64, 128], P(None, 'gx', 'gy'), may hold values 0 or 1
- leakage: float32 [64, 128, 128], P('gx', 'gy'), may hold values from 0.05 to 0.5
- source: float32 [64, 128, 128], P('gx', 'gy'), may hold values from -72 to 72
- weight: float32 [64, 128, 128], P('gx', 'gy'), may hold values from -72 to 72
Outputs:
- potential: float32 [64, 128, 128], P('gx', 'gy')
- adjoint: float32 [64, 128, 128], P('gx', 'gy')
- sensitivity: float32 [3, 64, 128, 128], P(None, 'gx', 'gy')
All inputs are finite; a program needn't handle non-finite values. No bound on the sum of `bond_mask` or of `electrode` on one device may be relied on, other than what follows from the above.
Results may differ from a plain program's by a relative error of at most 0.0003.
Values sent between devices are 32-bit elements; how exact they have to be, the bound alone decides.
A program may use at most 64 MiB of HBM per device.

v0:
```python
import jax
import jax.numpy as jnp
from jax import lax
from jax.sharding import PartitionSpec as P

ITERS = 4


def extended(block, sides, width):
    for axis, dim in sides:
        count = lax.axis_size(axis)
        forward = [(i, i + 1) for i in range(count - 1)]
        backward = [(target, source) for source, target in forward]
        low = lax.ppermute(
            lax.slice_in_dim(block, block.shape[dim] - width, None, axis=dim), axis, forward
        )
        high = lax.ppermute(lax.slice_in_dim(block, 0, width, axis=dim), axis, backward)
        block = jnp.concatenate([low, block, high], axis=dim)
    return block


def passed_along(value, axis, steps):
    count = lax.axis_size(axis)
    first, last = (max(0, -steps), min(count, count - steps))
    return lax.ppermute(value, axis, [(source, source + steps) for source in range(first, last)])


def totals(left, right):
    return jnp.sum(left * right, axis=(1, 2, 3))


def operate(fields, cond, below, diag):
    padded = extended(fields, (("gx", 1), ("gy", 2)), 1)
    up_x = padded[:, 2:, 1:-1]
    dn_x = padded[:, :-2, 1:-1]
    up_y = padded[:, 1:-1, 2:]
    dn_y = padded[:, 1:-1, :-2]
    zero_plane = jnp.zeros(fields.shape[:3] + (1,), jnp.float32)
    up_z = jnp.concatenate([fields[..., 1:], zero_plane], axis=3)
    dn_z = jnp.concatenate([zero_plane, fields[..., :-1]], axis=3)
    beside = (
        cond[0] * up_x
        + below[0] * dn_x
        + cond[1] * up_y
        + below[1] * dn_y
        + cond[2] * up_z
        + below[2] * dn_z
    )
    return diag * fields - beside


def precond_total(resid, scaled):
    return lax.psum(totals(resid, scaled), ("gx", "gy"))


def solve(rhs, cond, below, diag):
    solution = jnp.zeros_like(rhs)
    resid = rhs
    scaled = resid / diag
    direction = scaled
    norm_now = precond_total(resid, scaled)
    for step in range(ITERS):
        image = operate(direction, cond, below, diag)
        curv = lax.psum(totals(direction, image), ("gx", "gy"))
        alpha = (norm_now / curv)[:, None, None, None]
        solution = solution + alpha * direction
        resid = resid - alpha * image
        if step + 1 < ITERS:
            scaled = resid / diag
            fresh = precond_total(resid, scaled)
            direction = scaled + (fresh / norm_now)[:, None, None, None] * direction
            norm_now = fresh
    return solution


def body(bond_mask, levels, electrode, leakage, source, weight):
    cx, cy, nz = leakage.shape
    shape = (cx, cy, nz)
    row_x = lax.axis_index("gx") * cx + lax.broadcasted_iota(jnp.int32, (cx, 1, 1), 0)
    row_y = lax.axis_index("gy") * cy + lax.broadcasted_iota(jnp.int32, (1, cy, 1), 1)
    col_z = lax.broadcasted_iota(jnp.int32, (1, 1, nz), 2)
    inside = jnp.stack(
        [
            jnp.broadcast_to(row_x < cx * lax.axis_size("gx") - 1, shape),
            jnp.broadcast_to(row_y < cy * lax.axis_size("gy") - 1, shape),
            jnp.broadcast_to(col_z < nz - 1, shape),
        ]
    ).astype(jnp.float32)
    cond = (
        jnp.where(bond_mask == 1, levels[1][:, None, None, None], levels[0][:, None, None, None])
        * inside
    )
    rim_x = passed_along(cond[0, -1:], "gx", 1)
    rim_y = passed_along(cond[1, :, -1:], "gy", 1)
    below_x = jnp.concatenate([rim_x, cond[0, :-1]], axis=0)
    below_y = jnp.concatenate([rim_y, cond[1, :, :-1]], axis=1)
    below_z = jnp.concatenate([jnp.zeros((cx, cy, 1), jnp.float32), cond[2, :, :, :-1]], axis=2)
    below = (below_x, below_y, below_z)
    elec = electrode.astype(jnp.float32)
    first = jnp.where(col_z == 0, elec[0][:, :, None], 0.0)
    last = jnp.where(col_z == nz - 1, elec[1][:, :, None], 0.0)
    diag = leakage + first + last + cond[0] + cond[1] + cond[2] + below_x + below_y + below_z
    rhs = jnp.stack([source + first, weight + last])
    fields = jnp.concatenate(
        [solve(rhs[0:1], cond, below, diag), solve(rhs[1:2], cond, below, diag)], axis=0
    )
    next_x = passed_along(fields[:, :1], "gx", -1)
    next_y = passed_along(fields[:, :, :1], "gy", -1)
    up_x = jnp.concatenate([fields[:, 1:], next_x], axis=1)
    up_y = jnp.concatenate([fields[:, :, 1:], next_y], axis=2)
    up_z = jnp.concatenate([fields[..., 1:], jnp.zeros((2, cx, cy, 1), jnp.float32)], axis=3)
    potential = fields[0]
    adjoint = fields[1]
    sens = jnp.stack(
        [
            -(adjoint - ups[1]) * (potential - ups[0]) * inside[d]
            for d, ups in enumerate((up_x, up_y, up_z))
        ]
    )
    return (potential, adjoint, sens)


def solution(mesh):
    return jax.shard_map(
        body,
        mesh=mesh,
        in_specs=(
            P(None, "gx", "gy", None),
            P(),
            P(None, "gx", "gy"),
            P("gx", "gy", None),
            P("gx", "gy", None),
            P("gx", "gy", None),
        ),
        out_specs=(P("gx", "gy", None), P("gx", "gy", None), P(None, "gx", "gy", None)),
        check_vma=False,
    )
```

profile of v0, /device:TPU:0, one launch (start us, length us, event | category | flops | bytes accessed | tf_op | source)
XLA Modules:
  0.0 521.6 jit_solution(12219996019148539236)
XLA Ops:
  1.5 1.1 select_select_fusion
  2.7 2.4 collective-permute-start
  5.1 4.3 collective-permute-start.1
  10.7 0.8 multiply_reduce_fusion.13
  11.6 0.7 multiply_reduce_fusion.6
  12.4 3.1 collective-permute-start.19
  15.5 1.3 collective-permute-start.18
  16.9 3.2 collective-permute-start.3
  20.1 1.3 collective-permute-start.2
  21.4 1.3 collective-permute-start.20
  22.7 4.8 collective-permute-start.21
  27.6 1.3 collective-permute-start.4
  28.9 5.4 %collective-permute-start.5 = (f32[1,18,1,128]{3,2,1,0:T(1,128)S(1)}, f32[1,18,1,128]{3,2,1,0:T(1,128)S(1)}, u32[]{:S(2)}, u32[]{:S(2)}) collective-permute-start(f32[1,18,1,128]{3,2,1,0:T(1,128)S(1)} %get-tuple-element.60), channel_id=1, source_target_pairs={{0,1},{1,2},{2,3},{3,4},{4,5},{5,6},{6,7},{8,9},{9,10},{10,11},{11... | collective-permute-start | bytes 27656 | tf_op jit(solution)/shard_map/ppermute | solution.py:14
  34.4 0.8 multiply_reduce_fusion.5
  35.1 44.7 %all-reduce.23 = (f32[1]{0:T(128)}, f32[1]{0:T(128)}) all-reduce(f32[1]{0:T(128)} %bitcast.37, f32[1]{0:T(128)} %bitcast.40), channel_id=1, replica_groups=mesh['gx'=4,'gy'=8] {'gx','gy'}, use_global_device_ids=true, to_apply=%region_17.18 | all-reduce | flops 2 | bytes 16 | tf_op jit(solution)/shard_map/psum | solution.py:53
  81.2 0.8 multiply_reduce_fusion.4
  81.9 39.5 %psum.122 = f32[1]{0:T(128)} all-reduce(f32[1]{0:T(128)} %bitcast.44), channel_id=1, replica_groups=mesh['gx'=4,'gy'=8] {'gx','gy'}, use_global_device_ids=true, to_apply=%region_21.22 | all-reduce | flops 1 | bytes 8 | tf_op jit(solution)/shard_map/psum | solution.py:53
  122.8 1.3 collective-permute-start.23
  124.1 1.3 collective-permute-start.22
  125.4 0.8 multiply_reduce_fusion.12
  126.2 3.5 collective-permute-done.22
  129.7 1.3 collective-permute-start.24
  131.0 4.5 collective-permute-start.25
  135.6 1.2 collective-permute-done.25
  136.9 0.8 multiply_reduce_fusion.3
  137.7 42.8 %all-reduce.22 = (f32[1]{0:T(128)}, f32[1]{0:T(128)}, f32[1]{0:T(128)}) all-reduce(f32[1]{0:T(128)} %bitcast.47, f32[1]{0:T(128)} %bitcast.12, f32[1]{0:T(128)} %bitcast.18), channel_id=1, replica_groups=mesh['gx'=4,'gy'=8] {'gx','gy'}, use_global_device_ids=true, to_apply=%region_23.24 | all-reduce | flops 3 | bytes 24 | tf_op jit(solution)/shard_map/psum | solution.py:64
  183.1 0.7 multiply_reduce_fusion.2
  183.8 41.7 %all-reduce.21 = (f32[1]{0:T(128)}, f32[1]{0:T(128)}) all-reduce(f32[1]{0:T(128)} %bitcast.23, f32[1]{0:T(128)} %bitcast.49), channel_id=1, replica_groups=mesh['gx'=4,'gy'=8] {'gx','gy'}, use_global_device_ids=true, to_apply=%region_5.6 | all-reduce | flops 2 | bytes 16 | tf_op jit(solution)/shard_map/psum | solution.py:53
  228.3 1.3 collective-permute-start.27
  229.6 1.3 collective-permute-start.26
  231.0 5.5 %collective-permute-start.7 = (f32[1,1,16,128]{3,2,1,0:T(8,128)S(1)}, f32[1,1,16,128]{3,2,1,0:T(8,128)S(1)}, u32[]{:S(2)}, u32[]{:S(2)}) collective-permute-start(f32[1,1,16,128]{3,2,1,0:T(8,128)S(1)} %get-tuple-element.75), channel_id=1, source_target_pairs={{0,8},{8,16},{16,24},{1,9},{9,17},{17,25},{2,10},{10,18},{18,26},{... | collective-permute-start | bytes 24584 | tf_op jit(solution)/shard_map/ppermute | solution.py:14
  236.6 1.3 collective-permute-start.6
  237.9 1.3 collective-permute-start.28
  239.2 4.5 collective-permute-start.29
  243.8 1.3 collective-permute-start.8
  245.1 4.5 collective-permute-start.9
  249.7 0.8 multiply_reduce_fusion.1
  251.0 0.8 multiply_reduce_fusion.10
  251.8 44.0 %all-reduce.20 = (f32[1]{0:T(128)}, f32[1]{0:T(128)}) all-reduce(f32[1]{0:T(128)} %bitcast.51, f32[1]{0:T(128)} %bitcast.26), channel_id=1, replica_groups=mesh['gx'=4,'gy'=8] {'gx','gy'}, use_global_device_ids=true, to_apply=%region_27.28 | all-reduce | flops 2 | bytes 16 | tf_op jit(solution)/shard_map/psum | solution.py:64
  299.1 40.9 %psum.116 = f32[1]{0:T(128)} all-reduce(f32[1]{0:T(128)} %bitcast.28), channel_id=1, replica_groups=mesh['gx'=4,'gy'=8] {'gx','gy'}, use_global_device_ids=true, to_apply=%region_9.10 | all-reduce | flops 1 | bytes 8 | tf_op jit(solution)/shard_map/psum | solution.py:53
  341.5 1.3 collective-permute-start.11
  342.8 1.3 collective-permute-start.10
  344.1 4.2 collective-permute-done.10
  348.4 1.3 collective-permute-start.12
  349.7 4.5 collective-permute-start.13
  354.4 1.2 collective-permute-done.13
  355.6 0.8 multiply_reduce_fusion.8
  356.4 42.0 %psum.117 = f32[1]{0:T(128)} all-reduce(f32[1]{0:T(128)} %bitcast.30), channel_id=1, replica_groups=mesh['gx'=4,'gy'=8] {'gx','gy'}, use_global_device_ids=true, to_apply=%region_11.12 | all-reduce | flops 1 | bytes 8 | tf_op jit(solution)/shard_map/psum | solution.py:64
  400.5 40.3 %all-reduce.19 = (f32[1]{0:T(128)}, f32[1]{0:T(128)}) all-reduce(f32[1]{0:T(128)} %bitcast.32, f32[1]{0:T(128)} %bitcast.53), channel_id=1, replica_groups=mesh['gx'=4,'gy'=8] {'gx','gy'}, use_global_device_ids=true, to_apply=%region_13.14 | all-reduce | flops 2 | bytes 16 | tf_op jit(solution)/shard_map/psum | solution.py:53
  443.6 1.3 collective-permute-start.31
  444.9 1.3 collective-permute-start.30
  446.3 5.5 %collective-permute-start.15 = (f32[1,1,16,128]{3,2,1,0:T(8,128)S(1)}, f32[1,1,16,128]{3,2,1,0:T(8,128)S(1)}, u32[]{:S(2)}, u32[]{:S(2)}) collective-permute-start(f32[1,1,16,128]{3,2,1,0:T(8,128)S(1)} %get-tuple-element.69), channel_id=1, source_target_pairs={{0,8},{8,16},{16,24},{1,9},{9,17},{17,25},{2,10},{10,18},{18,26},{... | collective-permute-start | bytes 24584 | tf_op jit(solution)/shard_map/ppermute | solution.py:14
  451.9 1.3 collective-permute-start.14
  453.2 1.3 collective-permute-start.32
  454.5 4.5 collective-permute-start.33
  459.1 1.3 collective-permute-start.16
  460.4 4.5 collective-permute-start.17
  465.0 0.8 fusion.28
  466.3 0.7 fusion.70
  467.1 44.5 %all-reduce.18 = (f32[1]{0:T(128)}, f32[1]{0:T(128)}) all-reduce(f32[1]{0:T(128)} %bitcast.34, f32[1]{0:T(128)} %bitcast.55), channel_id=1, replica_groups=mesh['gx'=4,'gy'=8] {'gx','gy'}, use_global_device_ids=true, to_apply=%region_15.16 | all-reduce | flops 2 | bytes 16 | tf_op jit(solution)/shard_map/psum | solution.py:64
  514.6 1.3 collective-permute-start.35
  515.9 1.3 collective-permute-start.34
  517.2 3.5 collective-permute-done.35
  520.8 0.8 pad_maximum_fusion
  (99 shorter events, 6.3 us)
Async XLA Ops:
  0.7 0.7 copy-start.6
  2.7 7.4 %collective-permute-start = (f32[1,16,128]{2,1,0:T(8,128)S(1)}, f32[1,16,128]{2,1,0:T(8,128)S(1)}, u32[]{:S(2)}, u32[]{:S(2)}) collective-permute-start(f32[1,16,128]{2,1,0:T(8,128)S(1)} %slice_bitcast_fusion.4), channel_id=1, source_target_pairs={{0,8},{8,16},{16,24},{1,9},{9,17},{17,25},{2,10},{10,18},{18,26},{... | collective-permute-start | bytes 24584 | tf_op jit(solution)/shard_map/ppermute | solution.py:25
  5.1 5.6 %collective-permute-start.1 = (f32[16,1,128]{2,1,0:T(1,128)S(1)}, f32[16,1,128]{2,1,0:T(1,128)S(1)}, u32[]{:S(2)}, u32[]{:S(2)}) collective-permute-start(f32[16,1,128]{2,1,0:T(1,128)S(1)} %slice_bitcast_fusion.3), channel_id=1, source_target_pairs={{0,1},{1,2},{2,3},{3,4},{4,5},{5,6},{6,7},{8,9},{9,10},{10,11},{11... | collective-permute-start | bytes 24584 | tf_op jit(solution)/shard_map/ppermute | solution.py:25
  9.4 0.7 copy-start.5
  9.4 1.3 copy-start.3
  9.4 1.3 copy-start.4
  10.7 0.9 copy-start.2
  12.4 9.0 %collective-permute-start.19 = (f32[1,1,16,128]{3,2,1,0:T(8,128)S(1)}, f32[1,1,16,128]{3,2,1,0:T(8,128)S(1)}, u32[]{:S(2)}, u32[]{:S(2)}) collective-permute-start(f32[1,1,16,128]{3,2,1,0:T(8,128)S(1)} %get-tuple-element.89), channel_id=1, source_target_pairs={{0,8},{8,16},{16,24},{1,9},{9,17},{17,25},{2,10},{10,18},{18,26},{... | collective-permute-start | bytes 24584 | tf_op jit(solution)/shard_map/ppermute | solution.py:14
  15.5 5.9 %collective-permute-start.18 = (f32[1,1,16,128]{3,2,1,0:T(8,128)S(1)}, f32[1,1,16,128]{3,2,1,0:T(8,128)S(1)}, u32[]{:S(2)}, u32[]{:S(2)}) collective-permute-start(f32[1,1,16,128]{3,2,1,0:T(8,128)S(1)} %get-tuple-element.90), channel_id=1, source_target_pairs={{8,0},{16,8},{24,16},{9,1},{17,9},{25,17},{10,2},{18,10},{26,18},{... | collective-permute-start | bytes 24584 | tf_op jit(solution)/shard_map/ppermute | solution.py:17
  16.9 10.6 %collective-permute-start.3 = (f32[1,1,16,128]{3,2,1,0:T(8,128)S(1)}, f32[1,1,16,128]{3,2,1,0:T(8,128)S(1)}, u32[]{:S(2)}, u32[]{:S(2)}) collective-permute-start(f32[1,1,16,128]{3,2,1,0:T(8,128)S(1)} %get-tuple-element.93), channel_id=1, source_target_pairs={{0,8},{8,16},{16,24},{1,9},{9,17},{17,25},{2,10},{10,18},{18,26},{... | collective-permute-start | bytes 24584 | tf_op jit(solution)/shard_map/ppermute | solution.py:14
  20.1 7.5 %collective-permute-start.2 = (f32[1,1,16,128]{3,2,1,0:T(8,128)S(1)}, f32[1,1,16,128]{3,2,1,0:T(8,128)S(1)}, u32[]{:S(2)}, u32[]{:S(2)}) collective-permute-start(f32[1,1,16,128]{3,2,1,0:T(8,128)S(1)} %get-tuple-element.94), channel_id=1, source_target_pairs={{8,0},{16,8},{24,16},{9,1},{17,9},{25,17},{10,2},{18,10},{26,18},{... | collective-permute-start | bytes 24584 | tf_op jit(solution)/shard_map/ppermute | solution.py:17
  21.4 12.9 %collective-permute-start.20 = (f32[1,18,1,128]{3,2,1,0:T(1,128)S(1)}, f32[1,18,1,128]{3,2,1,0:T(1,128)S(1)}, u32[]{:S(2)}, u32[]{:S(2)}) collective-permute-start(f32[1,18,1,128]{3,2,1,0:T(1,128)S(1)} %get-tuple-element.57), channel_id=1, source_target_pairs={{1,0},{2,1},{3,2},{4,3},{5,4},{6,5},{7,6},{9,8},{10,9},{11,10},{12... | collective-permute-start | bytes 27656 | tf_op jit(solution)/shard_map/ppermute | solution.py:17
  22.7 11.6 %collective-permute-start.21 = (f32[1,18,1,128]{3,2,1,0:T(1,128)S(1)}, f32[1,18,1,128]{3,2,1,0:T(1,128)S(1)}, u32[]{:S(2)}, u32[]{:S(2)}) collective-permute-start(f32[1,18,1,128]{3,2,1,0:T(1,128)S(1)} %get-tuple-element.58), channel_id=1, source_target_pairs={{0,1},{1,2},{2,3},{3,4},{4,5},{5,6},{6,7},{8,9},{9,10},{10,11},{11... | collective-permute-start | bytes 27656 | tf_op jit(solution)/shard_map/ppermute | solution.py:14
  27.6 97.8 %collective-permute-start.4 = (f32[1,18,1,128]{3,2,1,0:T(1,128)S(1)}, f32[1,18,1,128]{3,2,1,0:T(1,128)S(1)}, u32[]{:S(2)}, u32[]{:S(2)}) collective-permute-start(f32[1,18,1,128]{3,2,1,0:T(1,128)S(1)} %get-tuple-element.59), channel_id=1, source_target_pairs={{1,0},{2,1},{3,2},{4,3},{5,4},{6,5},{7,6},{9,8},{10,9},{11,10},{12... | collective-permute-start | bytes 27656 | tf_op jit(solution)/shard_map/ppermute | solution.py:17
  28.9 96.5 %collective-permute-start.5 = (f32[1,18,1,128]{3,2,1,0:T(1,128)S(1)}, f32[1,18,1,128]{3,2,1,0:T(1,128)S(1)}, u32[]{:S(2)}, u32[]{:S(2)}) collective-permute-start(f32[1,18,1,128]{3,2,1,0:T(1,128)S(1)} %get-tuple-element.60), channel_id=1, source_target_pairs={{0,1},{1,2},{2,3},{3,4},{4,5},{5,6},{6,7},{8,9},{9,10},{10,11},{11... | collective-permute-start | bytes 27656 | tf_op jit(solution)/shard_map/ppermute | solution.py:14
  122.8 3.4 collective-permute-start.23
  124.1 5.6 %collective-permute-start.22 = (f32[1,1,16,128]{3,2,1,0:T(8,128)S(1)}, f32[1,1,16,128]{3,2,1,0:T(8,128)S(1)}, u32[]{:S(2)}, u32[]{:S(2)}) collective-permute-start(f32[1,1,16,128]{3,2,1,0:T(8,128)S(1)} %get-tuple-element.86), channel_id=1, source_target_pairs={{8,0},{16,8},{24,16},{9,1},{17,9},{25,17},{10,2},{18,10},{26,18},{... | collective-permute-start | bytes 24584 | tf_op jit(solution)/shard_map/ppermute | solution.py:17
  129.7 6.0 %collective-permute-start.24 = (f32[1,18,1,128]{3,2,1,0:T(1,128)S(1)}, f32[1,18,1,128]{3,2,1,0:T(1,128)S(1)}, u32[]{:S(2)}, u32[]{:S(2)}) collective-permute-start(f32[1,18,1,128]{3,2,1,0:T(1,128)S(1)} %get-tuple-element.55), channel_id=1, source_target_pairs={{1,0},{2,1},{3,2},{4,3},{5,4},{6,5},{7,6},{9,8},{10,9},{11,10},{12... | collective-permute-start | bytes 27656 | tf_op jit(solution)/shard_map/ppermute | solution.py:17
  131.0 5.9 %collective-permute-start.25 = (f32[1,18,1,128]{3,2,1,0:T(1,128)S(1)}, f32[1,18,1,128]{3,2,1,0:T(1,128)S(1)}, u32[]{:S(2)}, u32[]{:S(2)}) collective-permute-start(f32[1,18,1,128]{3,2,1,0:T(1,128)S(1)} %get-tuple-element.56), channel_id=1, source_target_pairs={{0,1},{1,2},{2,3},{3,4},{4,5},{5,6},{6,7},{8,9},{9,10},{10,11},{11... | collective-permute-start | bytes 27656 | tf_op jit(solution)/shard_map/ppermute | solution.py:14
  228.3 9.6 %collective-permute-start.27 = (f32[1,1,16,128]{3,2,1,0:T(8,128)S(1)}, f32[1,1,16,128]{3,2,1,0:T(8,128)S(1)}, u32[]{:S(2)}, u32[]{:S(2)}) collective-permute-start(f32[1,1,16,128]{3,2,1,0:T(8,128)S(1)} %get-tuple-element.79), channel_id=1, source_target_pairs={{0,8},{8,16},{16,24},{1,9},{9,17},{17,25},{2,10},{10,18},{18,26},{... | collective-permute-start | bytes 24584 | tf_op jit(solution)/shard_map/ppermute | solution.py:14
  229.6 8.3 %collective-permute-start.26 = (f32[1,1,16,128]{3,2,1,0:T(8,128)S(1)}, f32[1,1,16,128]{3,2,1,0:T(8,128)S(1)}, u32[]{:S(2)}, u32[]{:S(2)}) collective-permute-start(f32[1,1,16,128]{3,2,1,0:T(8,128)S(1)} %get-tuple-element.80), channel_id=1, source_target_pairs={{8,0},{16,8},{24,16},{9,1},{17,9},{25,17},{10,2},{18,10},{26,18},{... | collective-permute-start | bytes 24584 | tf_op jit(solution)/shard_map/ppermute | solution.py:17
  231.0 12.8 %collective-permute-start.7 = (f32[1,1,16,128]{3,2,1,0:T(8,128)S(1)}, f32[1,1,16,128]{3,2,1,0:T(8,128)S(1)}, u32[]{:S(2)}, u32[]{:S(2)}) collective-permute-start(f32[1,1,16,128]{3,2,1,0:T(8,128)S(1)} %get-tuple-element.75), channel_id=1, source_target_pairs={{0,8},{8,16},{16,24},{1,9},{9,17},{17,25},{2,10},{10,18},{18,26},{... | collective-permute-start | bytes 24584 | tf_op jit(solution)/shard_map/ppermute | solution.py:14
  236.6 7.2 %collective-permute-start.6 = (f32[1,1,16,128]{3,2,1,0:T(8,128)S(1)}, f32[1,1,16,128]{3,2,1,0:T(8,128)S(1)}, u32[]{:S(2)}, u32[]{:S(2)}) collective-permute-start(f32[1,1,16,128]{3,2,1,0:T(8,128)S(1)} %get-tuple-element.76), channel_id=1, source_target_pairs={{8,0},{16,8},{24,16},{9,1},{17,9},{25,17},{10,2},{18,10},{26,18},{... | collective-permute-start | bytes 24584 | tf_op jit(solution)/shard_map/ppermute | solution.py:17
  237.9 11.8 %collective-permute-start.28 = (f32[1,18,1,128]{3,2,1,0:T(1,128)S(1)}, f32[1,18,1,128]{3,2,1,0:T(1,128)S(1)}, u32[]{:S(2)}, u32[]{:S(2)}) collective-permute-start(f32[1,18,1,128]{3,2,1,0:T(1,128)S(1)} %get-tuple-element.53), channel_id=1, source_target_pairs={{1,0},{2,1},{3,2},{4,3},{5,4},{6,5},{7,6},{9,8},{10,9},{11,10},{12... | collective-permute-start | bytes 27656 | tf_op jit(solution)/shard_map/ppermute | solution.py:17
  239.2 10.5 %collective-permute-start.29 = (f32[1,18,1,128]{3,2,1,0:T(1,128)S(1)}, f32[1,18,1,128]{3,2,1,0:T(1,128)S(1)}, u32[]{:S(2)}, u32[]{:S(2)}) collective-permute-start(f32[1,18,1,128]{3,2,1,0:T(1,128)S(1)} %get-tuple-element.54), channel_id=1, source_target_pairs={{0,1},{1,2},{2,3},{3,4},{4,5},{5,6},{6,7},{8,9},{9,10},{10,11},{11... | collective-permute-start | bytes 27656 | tf_op jit(solution)/shard_map/ppermute | solution.py:14
  243.8 6.6 %collective-permute-start.8 = (f32[1,18,1,128]{3,2,1,0:T(1,128)S(1)}, f32[1,18,1,128]{3,2,1,0:T(1,128)S(1)}, u32[]{:S(2)}, u32[]{:S(2)}) collective-permute-start(f32[1,18,1,128]{3,2,1,0:T(1,128)S(1)} %get-tuple-element.51), channel_id=1, source_target_pairs={{1,0},{2,1},{3,2},{4,3},{5,4},{6,5},{7,6},{9,8},{10,9},{11,10},{12... | collective-permute-start | bytes 27656 | tf_op jit(solution)/shard_map/ppermute | solution.py:17
  245.1 5.9 %collective-permute-start.9 = (f32[1,18,1,128]{3,2,1,0:T(1,128)S(1)}, f32[1,18,1,128]{3,2,1,0:T(1,128)S(1)}, u32[]{:S(2)}, u32[]{:S(2)}) collective-permute-start(f32[1,18,1,128]{3,2,1,0:T(1,128)S(1)} %get-tuple-element.52), channel_id=1, source_target_pairs={{0,1},{1,2},{2,3},{3,4},{4,5},{5,6},{6,7},{8,9},{9,10},{10,11},{11... | collective-permute-start | bytes 27656 | tf_op jit(solution)/shard_map/ppermute | solution.py:14
  341.5 2.6 collective-permute-start.11
  342.8 5.6 %collective-permute-start.10 = (f32[1,1,16,128]{3,2,1,0:T(8,128)S(1)}, f32[1,1,16,128]{3,2,1,0:T(8,128)S(1)}, u32[]{:S(2)}, u32[]{:S(2)}) collective-permute-start(f32[1,1,16,128]{3,2,1,0:T(8,128)S(1)} %get-tuple-element.72), channel_id=1, source_target_pairs={{8,0},{16,8},{24,16},{9,1},{17,9},{25,17},{10,2},{18,10},{26,18},{... | collective-permute-start | bytes 24584 | tf_op jit(solution)/shard_map/ppermute | solution.py:17
  348.4 6.0 %collective-permute-start.12 = (f32[1,18,1,128]{3,2,1,0:T(1,128)S(1)}, f32[1,18,1,128]{3,2,1,0:T(1,128)S(1)}, u32[]{:S(2)}, u32[]{:S(2)}) collective-permute-start(f32[1,18,1,128]{3,2,1,0:T(1,128)S(1)} %get-tuple-element.49), channel_id=1, source_target_pairs={{1,0},{2,1},{3,2},{4,3},{5,4},{6,5},{7,6},{9,8},{10,9},{11,10},{12... | collective-permute-start | bytes 27656 | tf_op jit(solution)/shard_map/ppermute | solution.py:17
  349.7 5.9 %collective-permute-start.13 = (f32[1,18,1,128]{3,2,1,0:T(1,128)S(1)}, f32[1,18,1,128]{3,2,1,0:T(1,128)S(1)}, u32[]{:S(2)}, u32[]{:S(2)}) collective-permute-start(f32[1,18,1,128]{3,2,1,0:T(1,128)S(1)} %get-tuple-element.50), channel_id=1, source_target_pairs={{0,1},{1,2},{2,3},{3,4},{4,5},{5,6},{6,7},{8,9},{9,10},{10,11},{11... | collective-permute-start | bytes 27656 | tf_op jit(solution)/shard_map/ppermute | solution.py:14
  443.6 9.6 %collective-permute-start.31 = (f32[1,1,16,128]{3,2,1,0:T(8,128)S(1)}, f32[1,1,16,128]{3,2,1,0:T(8,128)S(1)}, u32[]{:S(2)}, u32[]{:S(2)}) collective-permute-start(f32[1,1,16,128]{3,2,1,0:T(8,128)S(1)} %get-tuple-element.63), channel_id=1, source_target_pairs={{0,8},{8,16},{16,24},{1,9},{9,17},{17,25},{2,10},{10,18},{18,26},{... | collective-permute-start | bytes 24584 | tf_op jit(solution)/shard_map/ppermute | solution.py:14
  444.9 8.3 %collective-permute-start.30 = (f32[1,1,16,128]{3,2,1,0:T(8,128)S(1)}, f32[1,1,16,128]{3,2,1,0:T(8,128)S(1)}, u32[]{:S(2)}, u32[]{:S(2)}) collective-permute-start(f32[1,1,16,128]{3,2,1,0:T(8,128)S(1)} %get-tuple-element.64), channel_id=1, source_target_pairs={{8,0},{16,8},{24,16},{9,1},{17,9},{25,17},{10,2},{18,10},{26,18},{... | collective-permute-start | bytes 24584 | tf_op jit(solution)/shard_map/ppermute | solution.py:17
  446.3 12.8 %collective-permute-start.15 = (f32[1,1,16,128]{3,2,1,0:T(8,128)S(1)}, f32[1,1,16,128]{3,2,1,0:T(8,128)S(1)}, u32[]{:S(2)}, u32[]{:S(2)}) collective-permute-start(f32[1,1,16,128]{3,2,1,0:T(8,128)S(1)} %get-tuple-element.69), channel_id=1, source_target_pairs={{0,8},{8,16},{16,24},{1,9},{9,17},{17,25},{2,10},{10,18},{18,26},{... | collective-permute-start | bytes 24584 | tf_op jit(solution)/shard_map/ppermute | solution.py:14
  451.9 7.2 %collective-permute-start.14 = (f32[1,1,16,128]{3,2,1,0:T(8,128)S(1)}, f32[1,1,16,128]{3,2,1,0:T(8,128)S(1)}, u32[]{:S(2)}, u32[]{:S(2)}) collective-permute-start(f32[1,1,16,128]{3,2,1,0:T(8,128)S(1)} %get-tuple-element.70), channel_id=1, source_target_pairs={{8,0},{16,8},{24,16},{9,1},{17,9},{25,17},{10,2},{18,10},{26,18},{... | collective-permute-start | bytes 24584 | tf_op jit(solution)/shard_map/ppermute | solution.py:17
  453.2 11.8 %collective-permute-start.32 = (f32[1,18,1,128]{3,2,1,0:T(1,128)S(1)}, f32[1,18,1,128]{3,2,1,0:T(1,128)S(1)}, u32[]{:S(2)}, u32[]{:S(2)}) collective-permute-start(f32[1,18,1,128]{3,2,1,0:T(1,128)S(1)} %get-tuple-element.45), channel_id=1, source_target_pairs={{1,0},{2,1},{3,2},{4,3},{5,4},{6,5},{7,6},{9,8},{10,9},{11,10},{12... | collective-permute-start | bytes 27656 | tf_op jit(solution)/shard_map/ppermute | solution.py:17
  454.5 10.5 %collective-permute-start.33 = (f32[1,18,1,128]{3,2,1,0:T(1,128)S(1)}, f32[1,18,1,128]{3,2,1,0:T(1,128)S(1)}, u32[]{:S(2)}, u32[]{:S(2)}) collective-permute-start(f32[1,18,1,128]{3,2,1,0:T(1,128)S(1)} %get-tuple-element.46), channel_id=1, source_target_pairs={{0,1},{1,2},{2,3},{3,4},{4,5},{5,6},{6,7},{8,9},{9,10},{10,11},{11... | collective-permute-start | bytes 27656 | tf_op jit(solution)/shard_map/ppermute | solution.py:14
  459.1 6.7 %collective-permute-start.16 = (f32[1,18,1,128]{3,2,1,0:T(1,128)S(1)}, f32[1,18,1,128]{3,2,1,0:T(1,128)S(1)}, u32[]{:S(2)}, u32[]{:S(2)}) collective-permute-start(f32[1,18,1,128]{3,2,1,0:T(1,128)S(1)} %get-tuple-element.47), channel_id=1, source_target_pairs={{1,0},{2,1},{3,2},{4,3},{5,4},{6,5},{7,6},{9,8},{10,9},{11,10},{12... | collective-permute-start | bytes 27656 | tf_op jit(solution)/shard_map/ppermute | solution.py:17
  460.4 5.9 %collective-permute-start.17 = (f32[1,18,1,128]{3,2,1,0:T(1,128)S(1)}, f32[1,18,1,128]{3,2,1,0:T(1,128)S(1)}, u32[]{:S(2)}, u32[]{:S(2)}) collective-permute-start(f32[1,18,1,128]{3,2,1,0:T(1,128)S(1)} %get-tuple-element.48), channel_id=1, source_target_pairs={{0,1},{1,2},{2,3},{3,4},{4,5},{5,6},{6,7},{8,9},{9,10},{10,11},{11... | collective-permute-start | bytes 27656 | tf_op jit(solution)/shard_map/ppermute | solution.py:14
  514.3 6.4 %copy-start = (f32[1,16,16,128]{3,2,1,0:T(8,128)}, f32[1,16,16,128]{3,2,1,0:T(8,128)S(1)}, u32[]{:S(2)}) copy-start(f32[1,16,16,128]{3,2,1,0:T(8,128)S(1)} %fusion.109) | copy-start | bytes 393220
  514.3 6.4 %copy-start.1 = (f32[1,16,16,128]{3,2,1,0:T(8,128)}, f32[1,16,16,128]{3,2,1,0:T(8,128)S(1)}, u32[]{:S(2)}) copy-start(f32[1,16,16,128]{3,2,1,0:T(8,128)S(1)} %fusion.107) | copy-start | bytes 393220
  514.6 6.2 %collective-permute-start.35 = (f32[2,16,1,128]{3,2,1,0:T(1,128)S(1)}, f32[2,16,1,128]{3,2,1,0:T(1,128)S(1)}, u32[]{:S(2)}, u32[]{:S(2)}) collective-permute-start(f32[2,16,1,128]{3,2,1,0:T(1,128)S(1)} %fusion.113), channel_id=1, source_target_pairs={{1,0},{2,1},{3,2},{4,3},{5,4},{6,5},{7,6},{9,8},{10,9},{11,10},{12... | collective-permute-start | bytes 49160 | tf_op jit(solution)/shard_map/ppermute | solution.py:25
  515.9 4.9 collective-permute-start.34
where the time goes:
time: 527 us; the launch traced here: 522 us
  blocking collectives  380 us (72%)
  starting transfers between devices  89.9 us (17%)
  between operations  20 us (4%)
  waiting for transfers between devices  15.5 us (3%)
  other arithmetic  13.4 us (3%)
    psum x5, blocking collectives, precond_total(): return lax.psum(totals(resid, scaled), ('gx', 'gy'))  207 us
    psum x4, blocking collectives, solve(): curv = lax.psum(totals(direction, image), ('gx', 'gy'))  173 us
    ppermute x16, starting transfers between devices, extended(): lax.ppermute(lax.slice_in_dim(block, block.shape[dim] - width, None, axis...  60 us
    ppermute x16, starting transfers between devices, extended(): lax.ppermute(lax.slice_in_dim(block, 0, width, axis=dim), axis, backward)  20.7 us
    reduce_sum x14, other arithmetic, totals(): return jnp.sum(left * right, axis=(1, 2, 3))  10.7 us
  transfers between devices with their start and end apart: 36, of which 8 were waited for; matrix products, arithmetic and copies ran while one was open for 1% of the time, Pallas kernels for 0%

commit v1 on v0

v1 whole, which is shorter than its diff:
```python
import functools

import jax
import jax.numpy as jnp
from jax import lax
from jax.experimental import pallas as pl
from jax.experimental.pallas import tpu as pltpu
from jax.sharding import PartitionSpec as P

ITERS = 4
MOMENTS = 2 * ITERS
MESH = pl.DeviceIdType.MESH
UNROLL = 16


def coefficients(mu):
    def norm(c):
        total = None
        for i in range(len(c)):
            for j in range(i, len(c)):
                term = c[i] * c[j] * mu[i + j]
                term = term if i == j else term + term
                total = term if total is None else total + term
        return total

    def curved(c):
        total = None
        for i in range(len(c)):
            for j in range(i, len(c)):
                term = c[i] * c[j] * (mu[i + j] - mu[i + j + 1])
                term = term if i == j else term + term
                total = term if total is None else total + term
        return total

    one = jnp.ones_like(mu[0])
    scaled, direction, answer = [one], [one], []
    norm_now = mu[0]
    for step in range(ITERS):
        alpha = norm_now / curved(direction)
        answer = [a + alpha * d for a, d in zip(answer, direction)] + [alpha * direction[-1]]
        if step + 1 < ITERS:
            image = [direction[0]]
            image += [b - a for a, b in zip(direction[:-1], direction[1:])]
            image += [-direction[-1]]
            scaled = [s - alpha * q for s, q in zip(scaled, image)] + [-alpha * image[-1]]
            fresh = norm(scaled)
            beta = fresh / norm_now
            direction = [s + beta * d for s, d in zip(scaled, direction)] + [scaled[-1]]
            norm_now = fresh
    return answer


def kernel(
    nx, ny,
    levels, mask_in, elec_in, leak_in, src_in, wgt_in,
    pot_out, adj_out, sens_out,
    mask, elec, leak, rhs, in_sem,
    cx, cy, by, cz, bz, inv,
    rim_x, rim_y, rim_y_send, rim_send, rim_recv,
    field, y_lo, y_hi, y_lo_send, y_hi_send, halo_send, halo_recv,
    part, part_x, sum_y, part_y, px_send, px_recv, py_send, py_recv,
    answer, sens, out_sem,
):
    bx, by_rows, nz = leak.shape
    ix, iy = lax.axis_index("gx"), lax.axis_index("gy")
    has_xl, has_xh = ix > 0, ix < nx - 1
    has_yl, has_yh = iy > 0, iy < ny - 1

    loads = [
        pltpu.make_async_copy(mask_in, mask, in_sem.at[0]),
        pltpu.make_async_copy(elec_in, elec, in_sem.at[1]),
        pltpu.make_async_copy(leak_in, leak, in_sem.at[2]),
        pltpu.make_async_copy(src_in, rhs.at[0], in_sem.at[3]),
        pltpu.make_async_copy(wgt_in, rhs.at[1], in_sem.at[4]),
    ]
    for load in loads:
        load.start()

    barrier = pltpu.get_barrier_semaphore()
    for k in range(1, nx):
        pl.semaphore_signal(barrier, inc=1, device_id={"gx": lax.rem(ix + k, nx)}, device_id_type=MESH)
    for k in range(1, ny):
        pl.semaphore_signal(barrier, inc=1, device_id={"gy": lax.rem(iy + k, ny)}, device_id_type=MESH)
    pl.semaphore_wait(barrier, nx + ny - 2)

    loads[0].wait()
    row = lax.broadcasted_iota(jnp.int32, (by_rows, nz), 0)
    lane = lax.broadcasted_iota(jnp.int32, (by_rows, nz), 1)
    rim_y_send[...] = mask[1, :, by_rows - 1 : by_rows, :]
    rim_copy_x = pltpu.make_async_remote_copy(
        mask.at[0, bx - 1], rim_x, rim_send.at[0], rim_recv.at[0],
        device_id={"gx": lax.rem(ix + 1, nx)}, device_id_type=MESH,
    )
    rim_copy_y = pltpu.make_async_remote_copy(
        rim_y_send, rim_y, rim_send.at[1], rim_recv.at[1],
        device_id={"gy": lax.rem(iy + 1, ny)}, device_id_type=MESH,
    )
    pl.when(has_xh)(rim_copy_x.start)
    pl.when(has_yh)(rim_copy_y.start)

    @pl.when(jnp.logical_not(has_xl))
    def _():
        rim_x[...] = jnp.zeros_like(rim_x)
        field[:, :, 0] = jnp.zeros_like(field[:, :, 0])

    @pl.when(jnp.logical_not(has_xh))
    def _():
        field[:, :, bx + 1] = jnp.zeros_like(field[:, :, bx + 1])

    @pl.when(jnp.logical_not(has_yl))
    def _():
        rim_y[...] = jnp.zeros_like(rim_y)
        y_lo[...] = jnp.zeros_like(y_lo)

    @pl.when(jnp.logical_not(has_yh))
    def _():
        y_hi[...] = jnp.zeros_like(y_hi)

    def conductance(bits, d):
        return jnp.where(bits == 1, levels[1, d], levels[0, d])

    x_low = has_xl.astype(jnp.float32)
    x_high = has_xh.astype(jnp.float32)
    y_low = has_yl.astype(jnp.float32)
    y_high = has_yh.astype(jnp.float32)
    not_last_row = jnp.where(row < by_rows - 1, 1.0, y_high)
    for load in loads[1:]:
        load.wait()
    square = (by_rows, by_rows)
    eye = lax.broadcasted_iota(jnp.int32, square, 0) == lax.broadcasted_iota(jnp.int32, square, 1)

    def column(which, x):
        line = elec[which, pl.ds(x, 1), :].astype(jnp.float32)
        return jnp.sum(jnp.where(eye, line, 0.0), axis=1, keepdims=True)

    def set_up(x, carry):
        here = conductance(mask[0, x], 0)
        cx[x + 1] = here * jnp.where(x < bx - 1, 1.0, x_high)
        here_y = conductance(mask[1, x], 1) * not_last_row
        cy[x] = here_y
        here_z = jnp.where(lane < nz - 1, conductance(mask[2, x], 2), 0.0)
        cz[x] = here_z
        back_z = pltpu.roll(here_z, 1, 1)
        bz[x] = back_z
        first = jnp.where(lane == 0, column(0, x), 0.0)
        last = jnp.where(lane == nz - 1, column(1, x), 0.0)
        rhs[0, x] = rhs[0, x] + first
        rhs[1, x] = rhs[1, x] + last
        leak[x] = leak[x] + first + last + cx[x + 1] + here_y + here_z + back_z
        return carry

    lax.fori_loop(0, bx, set_up, 0, unroll=UNROLL)
    pl.when(has_xl)(rim_copy_x.wait_recv)
    pl.when(has_yl)(rim_copy_y.wait_recv)
    cx[0] = conductance(rim_x[...], 0) * x_low

    def halos(k):
        return [
            (has_xl, has_xh, pltpu.make_async_remote_copy(
                field.at[k, :, 1], field.at[k, :, bx + 1], halo_send.at[k, 0], halo_recv.at[k, 0],
                device_id={"gx": lax.rem(ix + nx - 1, nx)}, device_id_type=MESH)),
            (has_xh, has_xl, pltpu.make_async_remote_copy(
                field.at[k, :, bx], field.at[k, :, 0], halo_send.at[k, 1], halo_recv.at[k, 1],
                device_id={"gx": lax.rem(ix + 1, nx)}, device_id_type=MESH)),
            (has_yl, has_yh, pltpu.make_async_remote_copy(
                y_lo_send.at[k], y_hi.at[k], halo_send.at[k, 2], halo_recv.at[k, 2],
                device_id={"gy": lax.rem(iy + ny - 1, ny)}, device_id_type=MESH)),
            (has_yh, has_yl, pltpu.make_async_remote_copy(
                y_hi_send.at[k], y_lo.at[k], halo_send.at[k, 3], halo_recv.at[k, 3],
                device_id={"gy": lax.rem(iy + 1, ny)}, device_id_type=MESH)),
        ]

    def put(k, f, x, value):
        field[k, f, x + 1] = value
        y_lo_send[k, f, x] = value[0:1]
        y_hi_send[k, f, x] = value[by_rows - 1 : by_rows]

    def fold(value):
        total = value[0:8]
        for at in range(8, by_rows, 8):
            total = total + value[at : at + 8]
        return total

    nought = jnp.zeros((8, nz), jnp.float32)

    def begin(x, sums):
        back_y = jnp.where(row == 0, conductance(rim_y[x], 1) * y_low, pltpu.roll(cy[x], 1, 0))
        by[x] = back_y
        scale = 1.0 / (leak[x] + cx[x] + back_y)
        inv[x] = scale
        out = []
        for f in range(2):
            value = rhs[f, x] * scale
            put(0, f, x, value)
            out.append(sums[f] + fold(rhs[f, x] * value))
        return tuple(out)

    moments = [lax.fori_loop(0, bx, begin, (nought, nought), unroll=UNROLL)]

    def beside(k, f, x):
        here = field[k, f, x + 1]
        up_y = jnp.where(row == by_rows - 1, y_hi[k, f, x], pltpu.roll(here, by_rows - 1, 0))
        dn_y = jnp.where(row == 0, y_lo[k, f, x], pltpu.roll(here, 1, 0))
        total = cx[x + 1] * field[k, f, x + 2] + cx[x] * field[k, f, x]
        total = total + (cy[x] * up_y + by[x] * dn_y)
        total = total + (cz[x] * pltpu.roll(here, nz - 1, 1) + bz[x] * pltpu.roll(here, 1, 1))
        return here, total

    for k in range(ITERS):
        copies = halos(k)
        for sends, _, copy in copies:
            pl.when(sends)(copy.start)
        for _, receives, copy in copies:
            pl.when(receives)(copy.wait_recv)

        def advance(x, sums, k=k):
            out = []
            for f in range(2):
                here, total = beside(k, f, x)
                out.append(sums[len(out)] + fold(here * total))
                if k + 1 < ITERS:
                    value = total * inv[x]
                    put(k + 1, f, x, value)
                    out.append(sums[len(out)] + fold(value * total))
            return tuple(out)

        count = 4 if k + 1 < ITERS else 2
        sums = lax.fori_loop(0, bx, advance, (nought,) * count, unroll=UNROLL)
        if k + 1 < ITERS:
            moments += [(sums[0], sums[2]), (sums[1], sums[3])]
        else:
            moments += [(sums[0], sums[1])]

    rows = 2 * MOMENTS
    pick = lax.broadcasted_iota(jnp.int32, (rows, nz), 0) == lax.broadcasted_iota(jnp.int32, (rows, nz), 1)
    lines = [jnp.sum(value, axis=0, keepdims=True) for pair in moments for value in pair]
    each = jnp.sum(jnp.concatenate(lines, axis=0), axis=1, keepdims=True)
    message = jnp.sum(jnp.where(pick, each, 0.0), axis=0, keepdims=True)

    part[...] = message
    part_x[ix] = message
    copies = []
    for k in range(1, nx):
        copies.append(pltpu.make_async_remote_copy(
            part, part_x.at[ix], px_send.at[k], px_recv.at[k],
            device_id={"gx": lax.rem(ix + k, nx)}, device_id_type=MESH))
    for copy in copies:
        copy.start()
    for copy in copies:
        copy.wait_recv()
    message = jnp.sum(part_x[...], axis=0)
    sum_y[...] = message
    part_y[iy] = message
    for k in range(1, ny):
        copy = pltpu.make_async_remote_copy(
            sum_y, part_y.at[iy], py_send.at[k], py_recv.at[k],
            device_id={"gy": lax.rem(iy + k, ny)}, device_id_type=MESH)
        copies.append(copy)
        copy.start()
    for copy in copies[nx - 1 :]:
        copy.wait_recv()
    message = jnp.sum(part_y[...], axis=0)

    square = jnp.sum(jnp.where(pick, message, 0.0), axis=1, keepdims=True)
    square = jnp.broadcast_to(square, (rows, nz))
    weights = coefficients([square[2 * k : 2 * k + 2] for k in range(MOMENTS)])
    weights = [[jnp.broadcast_to(w[f : f + 1], (by_rows, nz)) for w in weights] for f in range(2)]

    def combine(x, carry):
        for f in range(2):
            total = weights[f][0] * field[0, f, x + 1]
            for k in range(1, ITERS):
                total = total + weights[f][k] * field[k, f, x + 1]
            answer[f, x] = total
        return carry

    lax.fori_loop(0, bx + 1, combine, 0, unroll=UNROLL + 1)
    stores = [
        pltpu.make_async_copy(answer.at[0, pl.ds(0, bx)], pot_out, out_sem.at[0]),
        pltpu.make_async_copy(answer.at[1, pl.ds(0, bx)], adj_out, out_sem.at[1]),
    ]
    for store in stores:
        store.start()

    def differences(x, carry):
        gaps = []
        for f in range(2):
            here = answer[f, x]
            rim = weights[f][0][0:1] * y_hi[0, f, x]
            for k in range(1, ITERS):
                rim = rim + weights[f][k][0:1] * y_hi[k, f, x]
            up_y = jnp.where(row == by_rows - 1, rim, pltpu.roll(here, by_rows - 1, 0))
            gaps.append((here - answer[f, x + 1], here - up_y, here - pltpu.roll(here, nz - 1, 1)))
        sens[0, x] = -gaps[1][0] * gaps[0][0] * jnp.where(x < bx - 1, 1.0, x_high)
        sens[1, x] = -gaps[1][1] * gaps[0][1] * not_last_row
        sens[2, x] = jnp.where(lane < nz - 1, -gaps[1][2] * gaps[0][2], 0.0)
        return carry

    lax.fori_loop(0, bx, differences, 0, unroll=UNROLL)
    stores.append(pltpu.make_async_copy(sens, sens_out, out_sem.at[2]))
    stores[-1].start()

    pl.when(has_xh)(rim_copy_x.wait_send)
    pl.when(has_yh)(rim_copy_y.wait_send)
    for k in range(ITERS):
        for sends, _, copy in halos(k):
            pl.when(sends)(copy.wait_send)
    for copy in copies:
        copy.wait_send()
    for store in stores:
        store.wait()


def body(nx, ny, bond_mask, levels, electrode, leakage, source, weight):
    bx, by, nz = leakage.shape
    f32, i32 = jnp.float32, jnp.int32
    vmem, dma = pltpu.VMEM, pltpu.SemaphoreType.DMA
    block = (bx, by, nz)
    anywhere = pl.BlockSpec(memory_space=pl.ANY)
    return pl.pallas_call(
        functools.partial(kernel, nx, ny),
        out_shape=(
            jax.ShapeDtypeStruct(block, f32),
            jax.ShapeDtypeStruct(block, f32),
            jax.ShapeDtypeStruct((3,) + block, f32),
        ),
        in_specs=[pl.BlockSpec(memory_space=pltpu.SMEM)] + [anywhere] * 5,
        out_specs=[anywhere] * 3,
        scratch_shapes=[
            vmem((3,) + block, i32), vmem((2, bx, by), i32), vmem(block, f32), vmem((2,) + block, f32), dma((5,)),
            vmem((bx + 1, by, nz), f32), vmem(block, f32), vmem(block, f32), vmem(block, f32), vmem(block, f32),
            vmem(block, f32),
            vmem((by, nz), i32), vmem((bx, 1, nz), i32), vmem((bx, 1, nz), i32), dma((2,)), dma((2,)),
            vmem((ITERS, 2, bx + 2, by, nz), f32),
            vmem((ITERS, 2, bx, 1, nz), f32), vmem((ITERS, 2, bx, 1, nz), f32),
            vmem((ITERS, 2, bx, 1, nz), f32), vmem((ITERS, 2, bx, 1, nz), f32),
            dma((ITERS, 4)), dma((ITERS, 4)),
            vmem((1, nz), f32), vmem((nx, 1, nz), f32), vmem((1, nz), f32), vmem((ny, 1, nz), f32),
            dma((nx,)), dma((nx,)), dma((ny,)), dma((ny,)),
            vmem((2, bx + 1, by, nz), f32), vmem((3,) + block, f32), dma((3,)),
        ],
        compiler_params=pltpu.CompilerParams(
            collective_id=0, has_side_effects=True, vmem_limit_bytes=32 * 1024 * 1024
        ),
    )(levels, bond_mask, electrode, leakage, source, weight)


def solution(mesh):
    return jax.shard_map(
        functools.partial(body, mesh.shape["gx"], mesh.shape["gy"]),
        mesh=mesh,
        in_specs=(
            P(None, "gx", "gy", None),
            P(),
            P(None, "gx", "gy"),
            P("gx", "gy", None),
            P("gx", "gy", None),
            P("gx", "gy", None),
        ),
        out_specs=(P("gx", "gy", None), P("gx", "gy", None), P(None, "gx", "gy", None)),
        check_vma=False,
    )
```

time: 527 us -> 39.5 us (0.07)
  blocking collectives: 380 us -> 0 us
  starting transfers between devices: 89.9 us -> 0 us
  Pallas kernels: 0 us -> 31.4 us
  between operations: 20 us -> 0.65 us
  waiting for transfers between devices: 15.5 us -> 0 us
  other arithmetic: 13.4 us -> 0 us
    psum x9 -> x0, blocking collectives: 380 us -> none  [the longest x5 207 us: precond_total(): return lax.psum(totals(resid, scaled), ('gx', 'gy'))]
    ppermute x36 -> x0, starting transfers between devices: 89.9 us -> none  [the longest x16 60 us: extended(): lax.ppermute(lax.slice_in_dim(block, block.shape[dim] - width, None, axis...]
    pallas_call x0 -> x1, Pallas kernels: none -> 31.4 us  [body(): pl.pallas_call(functools.partial(kernel, nx, ny), out_shape=(jax.ShapeDty...]
    ppermute x36 -> x0, waiting for transfers between devices: 15.5 us -> none  [the longest x16 7.74 us: extended(): lax.ppermute(lax.slice_in_dim(block, 0, width, axis=dim), axis, backward)]
    reduce_sum x14 -> x0, other arithmetic: 10.7 us -> none  [totals(): return jnp.sum(left * right, axis=(1, 2, 3))]
    unnamed x14 -> x15, local copies, waits for them, and re-layouts: 1.45 us -> 7.15 us
  transfers between devices with their start and end apart: 36 -> 0, of which waited for: 8 -> 0; matrix products, arithmetic and copies ran while one was open for 1% -> 0% of each run, Pallas kernels for 0% -> 0%
where the time goes in v1:
time: 39.5 us; the launch traced here: 39.2 us
  Pallas kernels  31.4 us (79%)
  local copies, waits for them, and re-layouts  7.15 us (18%)
  between operations  0.65 us (2%)
    pallas_call x1, Pallas kernels, body(): pl.pallas_call(functools.partial(kernel, nx, ny), out_shape=(jax.ShapeDty...  31.4 us
    unnamed x15, local copies, waits for them, and re-layouts  7.15 us

profile of v1, /device:TPU:0, one launch (start us, length us, event | category | flops | bytes accessed | tf_op | source)
XLA Modules:
  0.0 39.2 jit_solution(5973831498198537490)
XLA Ops:
  0.6 0.0 copy-start
  0.6 1.0 %copy-done = s32[3,16,16,128]{3,2,1,0:T(8,128)S(1)} copy-done((s32[3,16,16,128]{3,2,1,0:T(8,128)S(1)}, s32[3,16,16,128]{3,2,1,0:T(8,128)}, u32[]{:S(2)}) %copy-start) | copy-done | bytes 393240
  1.6 0.0 copy-start.1
  1.6 0.9 %copy-done.1 = f32[16,16,128]{2,1,0:T(8,128)S(1)} copy-done((f32[16,16,128]{2,1,0:T(8,128)S(1)}, f32[16,16,128]{2,1,0:T(8,128)}, u32[]{:S(2)}) %copy-start.1) | copy-done | bytes 131096
  2.5 0.0 copy-start.2
  2.5 0.9 %copy-done.2 = f32[16,16,128]{2,1,0:T(8,128)S(1)} copy-done((f32[16,16,128]{2,1,0:T(8,128)S(1)}, f32[16,16,128]{2,1,0:T(8,128)}, u32[]{:S(2)}) %copy-start.2) | copy-done | bytes 131096
  3.4 0.0 copy-start.3
  3.4 0.9 %copy-done.3 = f32[16,16,128]{2,1,0:T(8,128)S(1)} copy-done((f32[16,16,128]{2,1,0:T(8,128)S(1)}, f32[16,16,128]{2,1,0:T(8,128)}, u32[]{:S(2)}) %copy-start.3) | copy-done | bytes 131096
  4.3 0.0 copy-start.4
  4.3 0.7 %copy-done.4 = s32[2,16,16]{2,1,0:T(8,128)S(1)} copy-done((s32[2,16,16]{2,1,0:T(8,128)S(1)}, s32[2,16,16]{2,1,0:T(8,128)}, u32[]{:S(2)}) %copy-start.4) | copy-done | bytes 2072
  5.1 0.0 copy-start.5
  5.1 0.7 %copy-done.5 = f32[2,3]{1,0:T(2,128)S(1)} copy-done((f32[2,3]{1,0:T(2,128)S(1)}, f32[2,3]{1,0:T(2,128)}, u32[]{:S(2)}) %copy-start.5) | copy-done | bytes 48
  5.7 31.4 %shard_map.85 = (f32[16,16,128]{2,1,0:T(8,128)S(1)}, f32[16,16,128]{2,1,0:T(8,128)S(1)}, f32[3,16,16,128]{3,2,1,0:T(8,128)S(1)}) custom-call(f32[2,3]{1,0:T(2,128)S(1)} %copy-done.5, s32[3,16,16,128]{3,2,1,0:T(8,128)S(1)} %copy-done, s32[2,16,16]{2,1,0:T(8,128)S(1)} %copy-done.4, f32[16,16,128]{2,1,0:T(8,128)S(1)} %copy-done.1, ...), custom_call_target="tpu_custom_call" | custom-call | tf_op jit(solution)/shard_map/pallas_call | solution.py:320
  37.2 0.7 %copy.12 = f32[16,16,128]{2,1,0:T(8,128)} copy(f32[16,16,128]{2,1,0:T(8,128)S(1)} %get-tuple-element.6) | data formatting | bytes 262144
  37.8 0.7 %copy.13 = f32[16,16,128]{2,1,0:T(8,128)} copy(f32[16,16,128]{2,1,0:T(8,128)S(1)} %get-tuple-element.7) | data formatting | bytes 262144
  38.5 0.7 %copy.14 = f32[3,16,16,128]{3,2,1,0:T(8,128)} copy(f32[3,16,16,128]{3,2,1,0:T(8,128)S(1)} %get-tuple-element.8) | data formatting | bytes 786432
Async XLA Ops:
  0.6 1.0 %copy-start = (s32[3,16,16,128]{3,2,1,0:T(8,128)S(1)}, s32[3,16,16,128]{3,2,1,0:T(8,128)}, u32[]{:S(2)}) copy-start(s32[3,16,16,128]{3,2,1,0:T(8,128)} %mask_in.1) | copy-start | bytes 1179652
  1.6 0.9 %copy-start.1 = (f32[16,16,128]{2,1,0:T(8,128)S(1)}, f32[16,16,128]{2,1,0:T(8,128)}, u32[]{:S(2)}) copy-start(f32[16,16,128]{2,1,0:T(8,128)} %leak_in.1) | copy-start | bytes 393220
  2.5 0.9 %copy-start.2 = (f32[16,16,128]{2,1,0:T(8,128)S(1)}, f32[16,16,128]{2,1,0:T(8,128)}, u32[]{:S(2)}) copy-start(f32[16,16,128]{2,1,0:T(8,128)} %src_in.1) | copy-start | bytes 393220
  3.4 0.9 %copy-start.3 = (f32[16,16,128]{2,1,0:T(8,128)S(1)}, f32[16,16,128]{2,1,0:T(8,128)}, u32[]{:S(2)}) copy-start(f32[16,16,128]{2,1,0:T(8,128)} %wgt_in.1) | copy-start | bytes 393220
  4.3 0.7 %copy-start.4 = (s32[2,16,16]{2,1,0:T(8,128)S(1)}, s32[2,16,16]{2,1,0:T(8,128)}, u32[]{:S(2)}) copy-start(s32[2,16,16]{2,1,0:T(8,128)} %elec_in.1) | copy-start | bytes 6148
  5.1 0.7 %copy-start.5 = (f32[2,3]{1,0:T(2,128)S(1)}, f32[2,3]{1,0:T(2,128)}, u32[]{:S(2)}) copy-start(f32[2,3]{1,0:T(2,128)} %levels.1) | copy-start | bytes 76

commit v2 on v1

--- a/solution.py
+++ b/solution.py
@@ -11,6 +11,7 @@
 MOMENTS = 2 * ITERS
 MESH = pl.DeviceIdType.MESH
 UNROLL = 16
+VMEM_LIMIT = 62 * 1024 * 1024
 
 
 def coefficients(mu):
@@ -53,13 +54,13 @@
 def kernel(
     nx, ny,
     levels, mask_in, elec_in, leak_in, src_in, wgt_in,
-    pot_out, adj_out, sens_out,
+    answer_out, rims_out,
     mask, elec, leak, rhs, in_sem,
     cx, cy, by, cz, bz, inv,
     rim_x, rim_y, rim_y_send, rim_send, rim_recv,
     field, y_lo, y_hi, y_lo_send, y_hi_send, halo_send, halo_recv,
     part, part_x, sum_y, part_y, px_send, px_recv, py_send, py_recv,
-    answer, sens, out_sem,
+    answer, rims, out_sem,
 ):
     bx, by_rows, nz = leak.shape
     ix, iy = lax.axis_index("gx"), lax.axis_index("gy")
@@ -172,8 +173,8 @@
 
     def put(k, f, x, value):
         field[k, f, x + 1] = value
-        y_lo_send[k, f, x] = value[0:1]
-        y_hi_send[k, f, x] = value[by_rows - 1 : by_rows]
+        y_lo_send[k, f, pl.ds(x, 1), :] = value[0:1]
+        y_hi_send[k, f, pl.ds(x, 1), :] = value[by_rows - 1 : by_rows]
 
     def fold(value):
         total = value[0:8]
@@ -199,8 +200,8 @@
 
     def beside(k, f, x):
         here = field[k, f, x + 1]
-        up_y = jnp.where(row == by_rows - 1, y_hi[k, f, x], pltpu.roll(here, by_rows - 1, 0))
-        dn_y = jnp.where(row == 0, y_lo[k, f, x], pltpu.roll(here, 1, 0))
+        up_y = jnp.where(row == by_rows - 1, y_hi[k, f, pl.ds(x, 1), :], pltpu.roll(here, by_rows - 1, 0))
+        dn_y = jnp.where(row == 0, y_lo[k, f, pl.ds(x, 1), :], pltpu.roll(here, 1, 0))
         total = cx[x + 1] * field[k, f, x + 2] + cx[x] * field[k, f, x]
         total = total + (cy[x] * up_y + by[x] * dn_y)
         total = total + (cz[x] * pltpu.roll(here, nz - 1, 1) + bz[x] * pltpu.roll(here, 1, 1))
@@ -275,30 +276,17 @@
         return carry
 
     lax.fori_loop(0, bx + 1, combine, 0, unroll=UNROLL + 1)
+    for f in range(2):
+        rim = weights[f][0] * y_hi[0, f]
+        for k in range(1, ITERS):
+            rim = rim + weights[f][k] * y_hi[k, f]
+        rims[f] = rim
     stores = [
-        pltpu.make_async_copy(answer.at[0, pl.ds(0, bx)], pot_out, out_sem.at[0]),
-        pltpu.make_async_copy(answer.at[1, pl.ds(0, bx)], adj_out, out_sem.at[1]),
+        pltpu.make_async_copy(answer, answer_out, out_sem.at[0]),
+        pltpu.make_async_copy(rims, rims_out, out_sem.at[1]),
     ]
     for store in stores:
         store.start()
-
-    def differences(x, carry):
-        gaps = []
-        for f in range(2):
-            here = answer[f, x]
-            rim = weights[f][0][0:1] * y_hi[0, f, x]
-            for k in range(1, ITERS):
-                rim = rim + weights[f][k][0:1] * y_hi[k, f, x]
-            up_y = jnp.where(row == by_rows - 1, rim, pltpu.roll(here, by_rows - 1, 0))
-            gaps.append((here - answer[f, x + 1], here - up_y, here - pltpu.roll(here, nz - 1, 1)))
-        sens[0, x] = -gaps[1][0] * gaps[0][0] * jnp.where(x < bx - 1, 1.0, x_high)
-        sens[1, x] = -gaps[1][1] * gaps[0][1] * not_last_row
-        sens[2, x] = jnp.where(lane < nz - 1, -gaps[1][2] * gaps[0][2], 0.0)
-        return carry
-
-    lax.fori_loop(0, bx, differences, 0, unroll=UNROLL)
-    stores.append(pltpu.make_async_copy(sens, sens_out, out_sem.at[2]))
-    stores[-1].start()
 
     pl.when(has_xh)(rim_copy_x.wait_send)
     pl.when(has_yh)(rim_copy_y.wait_send)
@@ -311,38 +299,90 @@
         store.wait()
 
 
+def finish(nx, ny, answer_in, rims_in, pot_out, adj_out, sens_out, answer, rims, sens, in_sem, out_sem):
+    bx, by_rows, nz = pot_out.shape
+    loads = [
+        pltpu.make_async_copy(answer_in, answer, in_sem.at[0]),
+        pltpu.make_async_copy(rims_in, rims, in_sem.at[1]),
+    ]
+    stores = [
+        pltpu.make_async_copy(answer_in.at[0, pl.ds(0, bx)], pot_out, out_sem.at[0]),
+        pltpu.make_async_copy(answer_in.at[1, pl.ds(0, bx)], adj_out, out_sem.at[1]),
+    ]
+    for copy in loads + stores:
+        copy.start()
+    row = lax.broadcasted_iota(jnp.int32, (by_rows, nz), 0)
+    lane = lax.broadcasted_iota(jnp.int32, (by_rows, nz), 1)
+    x_high = (lax.axis_index("gx") < nx - 1).astype(jnp.float32)
+    y_high = (lax.axis_index("gy") < ny - 1).astype(jnp.float32)
+    not_last_row = jnp.where(row < by_rows - 1, 1.0, y_high)
+
+    for load in loads:
+        load.wait()
+
+    def differences(x, carry):
+        gaps = []
+        for f in range(2):
+            here = answer[f, x]
+            up_y = jnp.where(row == by_rows - 1, rims[f, pl.ds(x, 1), :], pltpu.roll(here, by_rows - 1, 0))
+            gaps.append((here - answer[f, x + 1], here - up_y, here - pltpu.roll(here, nz - 1, 1)))
+        sens[0, x] = -gaps[1][0] * gaps[0][0] * jnp.where(x < bx - 1, 1.0, x_high)
+        sens[1, x] = -gaps[1][1] * gaps[0][1] * not_last_row
+        sens[2, x] = jnp.where(lane < nz - 1, -gaps[1][2] * gaps[0][2], 0.0)
+        return carry
+
+    lax.fori_loop(0, bx, differences, 0, unroll=UNROLL)
+    stores.append(pltpu.make_async_copy(sens, sens_out, out_sem.at[2]))
+    stores[-1].start()
+    for store in stores:
+        store.wait()
+
+
 def body(nx, ny, bond_mask, levels, electrode, leakage, source, weight):
     bx, by, nz = leakage.shape
     f32, i32 = jnp.float32, jnp.int32
     vmem, dma = pltpu.VMEM, pltpu.SemaphoreType.DMA
     block = (bx, by, nz)
-    anywhere = pl.BlockSpec(memory_space=pl.ANY)
-    return pl.pallas_call(
+    hbm = pl.BlockSpec(memory_space=pltpu.HBM)
+    answer, rims = pl.pallas_call(
         functools.partial(kernel, nx, ny),
         out_shape=(
-            jax.ShapeDtypeStruct(block, f32),
-            jax.ShapeDtypeStruct(block, f32),
-            jax.ShapeDtypeStruct((3,) + block, f32),
+            jax.ShapeDtypeStruct((2, bx + 1, by, nz), f32),
+            jax.ShapeDtypeStruct((2, bx, nz), f32),
         ),
-        in_specs=[pl.BlockSpec(memory_space=pltpu.SMEM)] + [anywhere] * 5,
-        out_specs=[anywhere] * 3,
+        in_specs=[pl.BlockSpec(memory_space=pltpu.SMEM)] + [hbm] * 5,
+        out_specs=[hbm] * 2,
         scratch_shapes=[
             vmem((3,) + block, i32), vmem((2, bx, by), i32), vmem(block, f32), vmem((2,) + block, f32), dma((5,)),
             vmem((bx + 1, by, nz), f32), vmem(block, f32), vmem(block, f32), vmem(block, f32), vmem(block, f32),
             vmem(block, f32),
             vmem((by, nz), i32), vmem((bx, 1, nz), i32), vmem((bx, 1, nz), i32), dma((2,)), dma((2,)),
             vmem((ITERS, 2, bx + 2, by, nz), f32),
-            vmem((ITERS, 2, bx, 1, nz), f32), vmem((ITERS, 2, bx, 1, nz), f32),
-            vmem((ITERS, 2, bx, 1, nz), f32), vmem((ITERS, 2, bx, 1, nz), f32),
+            vmem((ITERS, 2, bx, nz), f32), vmem((ITERS, 2, bx, nz), f32),
+            vmem((ITERS, 2, bx, nz), f32), vmem((ITERS, 2, bx, nz), f32),
             dma((ITERS, 4)), dma((ITERS, 4)),
             vmem((1, nz), f32), vmem((nx, 1, nz), f32), vmem((1, nz), f32), vmem((ny, 1, nz), f32),
             dma((nx,)), dma((nx,)), dma((ny,)), dma((ny,)),
-            vmem((2, bx + 1, by, nz), f32), vmem((3,) + block, f32), dma((3,)),
+            vmem((2, bx + 1, by, nz), f32), vmem((2, bx, nz), f32), dma((2,)),
         ],
         compiler_params=pltpu.CompilerParams(
-            collective_id=0, has_side_effects=True, vmem_limit_bytes=32 * 1024 * 1024
+            collective_id=0, has_side_effects=True, vmem_limit_bytes=VMEM_LIMIT
         ),
     )(levels, bond_mask, electrode, leakage, source, weight)
+    return pl.pallas_call(
+        functools.partial(finish, nx, ny),
+        out_shape=(
+            jax.ShapeDtypeStruct(block, f32),
+            jax.ShapeDtypeStruct(block, f32),
+            jax.ShapeDtypeStruct((3,) + block, f32),
+        ),
+        in_specs=[hbm] * 2,
+        out_specs=[hbm] * 3,
+        scratch_shapes=[
+            vmem((2, bx + 1, by, nz), f32), vmem((2, bx, nz), f32), vmem((3,) + block, f32), dma((2,)), dma((3,)),
+        ],
+        compiler_params=pltpu.CompilerParams(vmem_limit_bytes=VMEM_LIMIT),
+    )(answer, rims)
 
 
 def solution(mesh):

time: 39.5 us -> 40.6 us (1.028)
  Pallas kernels: 31.4 us -> 39.8 us
  local copies, waits for them, and re-layouts: 7.15 us -> 0 us
    pallas_call x0 -> x1, Pallas kernels: none -> 9.09 us  [body(): pl.pallas_call(functools.partial(finish, nx, ny), out_shape=(jax.ShapeDty...]
    unnamed x15 -> x0, local copies, waits for them, and re-layouts: 7.15 us -> none
    pallas_call x1, Pallas kernels: 31.4 us -> 30.7 us  [body(): pl.pallas_call(functools.partial(kernel, nx, ny), out_shape=(jax.ShapeDty...]
where the time goes in v2:
time: 40.6 us; the launch traced here: 40.5 us
  Pallas kernels  39.8 us (98%)
  between operations  0.64 us (2%)
    pallas_call x1, Pallas kernels, body(): pl.pallas_call(functools.partial(kernel, nx, ny), out_shape=(jax.ShapeDty...  30.7 us
    pallas_call x1, Pallas kernels, body(): pl.pallas_call(functools.partial(finish, nx, ny), out_shape=(jax.ShapeDty...  9.09 us

profile of v2, /device:TPU:0, one launch (start us, length us, event | category | flops | bytes accessed | tf_op | source)
XLA Modules:
  0.0 40.5 jit_solution(2122411428990398805)
XLA Ops:
  0.6 30.7 %shard_map.85 = (f32[2,17,16,128]{3,2,1,0:T(8,128)}, f32[2,16,128]{2,1,0:T(8,128)}) custom-call(f32[2,3]{1,0:T(2,128)} %levels.1, s32[3,16,16,128]{3,2,1,0:T(8,128)} %mask_in.1, s32[2,16,16]{2,1,0:T(8,128)} %elec_in.1, f32[16,16,128]{2,1,0:T(8,128)} %leak_in.1, f32[16,16,128]{2,1,0:T(8,128)} %src_in.1, f32[16,16,128]{2,1,0:T(8,128)} %wgt_in.1), custom_call_target="tpu_custom_call" | custom-call | tf_op jit(solution)/shard_map/pallas_call | solution.py:347
  31.4 9.1 %shard_map.86 = (f32[16,16,128]{2,1,0:T(8,128)}, f32[16,16,128]{2,1,0:T(8,128)}, f32[3,16,16,128]{3,2,1,0:T(8,128)}) custom-call(f32[2,17,16,128]{3,2,1,0:T(8,128)} %get-tuple-element.5.answer_in, f32[2,16,128]{2,1,0:T(8,128)} %get-tuple-element.6.rims_in), custom_call_target="tpu_custom_call" | custom-call | tf_op jit(solution)/shard_map/pallas_call | solution.py:372

commit v3 on v1

--- a/solution.py
+++ b/solution.py
@@ -10,7 +10,8 @@
 ITERS = 4
 MOMENTS = 2 * ITERS
 MESH = pl.DeviceIdType.MESH
-UNROLL = 16
+UNROLL = 4
+VMEM_LIMIT = 62 * 1024 * 1024
 
 
 def coefficients(mu):
@@ -59,7 +60,7 @@
     rim_x, rim_y, rim_y_send, rim_send, rim_recv,
     field, y_lo, y_hi, y_lo_send, y_hi_send, halo_send, halo_recv,
     part, part_x, sum_y, part_y, px_send, px_recv, py_send, py_recv,
-    answer, sens, out_sem,
+    answer, rims, sens, out_sem,
 ):
     bx, by_rows, nz = leak.shape
     ix, iy = lax.axis_index("gx"), lax.axis_index("gy")
@@ -172,8 +173,8 @@
 
     def put(k, f, x, value):
         field[k, f, x + 1] = value
-        y_lo_send[k, f, x] = value[0:1]
-        y_hi_send[k, f, x] = value[by_rows - 1 : by_rows]
+        y_lo_send[k, f, pl.ds(x, 1), :] = value[0:1]
+        y_hi_send[k, f, pl.ds(x, 1), :] = value[by_rows - 1 : by_rows]
 
     def fold(value):
         total = value[0:8]
@@ -199,8 +200,8 @@
 
     def beside(k, f, x):
         here = field[k, f, x + 1]
-        up_y = jnp.where(row == by_rows - 1, y_hi[k, f, x], pltpu.roll(here, by_rows - 1, 0))
-        dn_y = jnp.where(row == 0, y_lo[k, f, x], pltpu.roll(here, 1, 0))
+        up_y = jnp.where(row == by_rows - 1, y_hi[k, f, pl.ds(x, 1), :], pltpu.roll(here, by_rows - 1, 0))
+        dn_y = jnp.where(row == 0, y_lo[k, f, pl.ds(x, 1), :], pltpu.roll(here, 1, 0))
         total = cx[x + 1] * field[k, f, x + 2] + cx[x] * field[k, f, x]
         total = total + (cy[x] * up_y + by[x] * dn_y)
         total = total + (cz[x] * pltpu.roll(here, nz - 1, 1) + bz[x] * pltpu.roll(here, 1, 1))
@@ -274,22 +275,25 @@
             answer[f, x] = total
         return carry
 
-    lax.fori_loop(0, bx + 1, combine, 0, unroll=UNROLL + 1)
+    lax.fori_loop(0, bx + 1, combine, 0, unroll=UNROLL)
+    for f in range(2):
+        rim = weights[f][0] * y_hi[0, f]
+        for k in range(1, ITERS):
+            rim = rim + weights[f][k] * y_hi[k, f]
+        rims[f] = rim
     stores = [
         pltpu.make_async_copy(answer.at[0, pl.ds(0, bx)], pot_out, out_sem.at[0]),
         pltpu.make_async_copy(answer.at[1, pl.ds(0, bx)], adj_out, out_sem.at[1]),
+        pltpu.make_async_copy(sens, sens_out, out_sem.at[2]),
     ]
-    for store in stores:
-        store.start()
+    stores[0].start()
+    stores[1].start()
 
     def differences(x, carry):
         gaps = []
         for f in range(2):
             here = answer[f, x]
-            rim = weights[f][0][0:1] * y_hi[0, f, x]
-            for k in range(1, ITERS):
-                rim = rim + weights[f][k][0:1] * y_hi[k, f, x]
-            up_y = jnp.where(row == by_rows - 1, rim, pltpu.roll(here, by_rows - 1, 0))
+            up_y = jnp.where(row == by_rows - 1, rims[f, pl.ds(x, 1), :], pltpu.roll(here, by_rows - 1, 0))
             gaps.append((here - answer[f, x + 1], here - up_y, here - pltpu.roll(here, nz - 1, 1)))
         sens[0, x] = -gaps[1][0] * gaps[0][0] * jnp.where(x < bx - 1, 1.0, x_high)
         sens[1, x] = -gaps[1][1] * gaps[0][1] * not_last_row
@@ -297,8 +301,7 @@
         return carry
 
     lax.fori_loop(0, bx, differences, 0, unroll=UNROLL)
-    stores.append(pltpu.make_async_copy(sens, sens_out, out_sem.at[2]))
-    stores[-1].start()
+    stores[2].start()
 
     pl.when(has_xh)(rim_copy_x.wait_send)
     pl.when(has_yh)(rim_copy_y.wait_send)
@@ -316,7 +319,7 @@
     f32, i32 = jnp.float32, jnp.int32
     vmem, dma = pltpu.VMEM, pltpu.SemaphoreType.DMA
     block = (bx, by, nz)
-    anywhere = pl.BlockSpec(memory_space=pl.ANY)
+    hbm = pl.BlockSpec(memory_space=pltpu.HBM)
     return pl.pallas_call(
         functools.partial(kernel, nx, ny),
         out_shape=(
@@ -324,23 +327,23 @@
             jax.ShapeDtypeStruct(block, f32),
             jax.ShapeDtypeStruct((3,) + block, f32),
         ),
-        in_specs=[pl.BlockSpec(memory_space=pltpu.SMEM)] + [anywhere] * 5,
-        out_specs=[anywhere] * 3,
+        in_specs=[pl.BlockSpec(memory_space=pltpu.SMEM)] + [hbm] * 5,
+        out_specs=[hbm] * 3,
         scratch_shapes=[
             vmem((3,) + block, i32), vmem((2, bx, by), i32), vmem(block, f32), vmem((2,) + block, f32), dma((5,)),
             vmem((bx + 1, by, nz), f32), vmem(block, f32), vmem(block, f32), vmem(block, f32), vmem(block, f32),
             vmem(block, f32),
             vmem((by, nz), i32), vmem((bx, 1, nz), i32), vmem((bx, 1, nz), i32), dma((2,)), dma((2,)),
             vmem((ITERS, 2, bx + 2, by, nz), f32),
-            vmem((ITERS, 2, bx, 1, nz), f32), vmem((ITERS, 2, bx, 1, nz), f32),
-            vmem((ITERS, 2, bx, 1, nz), f32), vmem((ITERS, 2, bx, 1, nz), f32),
+            vmem((ITERS, 2, bx, nz), f32), vmem((ITERS, 2, bx, nz), f32),
+            vmem((ITERS, 2, bx, nz), f32), vmem((ITERS, 2, bx, nz), f32),
             dma((ITERS, 4)), dma((ITERS, 4)),
             vmem((1, nz), f32), vmem((nx, 1, nz), f32), vmem((1, nz), f32), vmem((ny, 1, nz), f32),
             dma((nx,)), dma((nx,)), dma((ny,)), dma((ny,)),
-            vmem((2, bx + 1, by, nz), f32), vmem((3,) + block, f32), dma((3,)),
+            vmem((2, bx + 1, by, nz), f32), vmem((2, bx, nz), f32), vmem((3,) + block, f32), dma((3,)),
         ],
         compiler_params=pltpu.CompilerParams(
-            collective_id=0, has_side_effects=True, vmem_limit_bytes=32 * 1024 * 1024
+            collective_id=0, has_side_effects=True, vmem_limit_bytes=VMEM_LIMIT
         ),
     )(levels, bond_mask, electrode, leakage, source, weight)
 

time: 39.5 us -> 36.8 us (0.932)
  local copies, waits for them, and re-layouts: 7.15 us -> 3.93 us
  Pallas kernels: 31.4 us -> 32.1 us
    unnamed x15 -> x5, local copies, waits for them, and re-layouts: 7.15 us -> 3.93 us
    pallas_call x1, Pallas kernels: 31.4 us -> 32.1 us  [body(): pl.pallas_call(functools.partial(kernel, nx, ny), out_shape=(jax.ShapeDty...]
where the time goes in v3:
time: 36.8 us; the launch traced here: 36.6 us
  Pallas kernels  32.1 us (87%)
  local copies, waits for them, and re-layouts  3.93 us (11%)
  between operations  0.65 us (2%)
    pallas_call x1, Pallas kernels, body(): pl.pallas_call(functools.partial(kernel, nx, ny), out_shape=(jax.ShapeDty...  32.1 us
    unnamed x5, local copies, waits for them, and re-layouts  3.93 us

profile of v3, /device:TPU:0, one launch (start us, length us, event | category | flops | bytes accessed | tf_op | source)
XLA Modules:
  0.0 36.6 jit_solution(14122616599238305570)
XLA Ops:
  0.6 32.1 %shard_map.85 = (f32[16,16,128]{2,1,0:T(8,128)}, f32[16,16,128]{2,1,0:T(8,128)}, f32[3,16,16,128]{3,2,1,0:T(8,128)}) custom-call(f32[2,3]{1,0:T(2,128)} %levels.1, s32[3,16,16,128]{3,2,1,0:T(8,128)} %mask_in.1, s32[2,16,16]{2,1,0:T(8,128)} %elec_in.1, f32[16,16,128]{2,1,0:T(8,128)} %leak_in.1, f32[16,16,128]{2,1,0:T(8,128)} %src_in.1, f32[16,16,128]{2,1,0:T(8,128)} %wgt_in.1), custom_call_target="tpu_custom_call" | custom-call | tf_op jit(solution)/shard_map/pallas_call | solution.py:323
  32.7 0.0 copy-start
  32.7 1.6 %copy.12 = f32[16,16,128]{2,1,0:T(8,128)} copy(f32[16,16,128]{2,1,0:T(8,128)} %get-tuple-element.6) | data formatting | bytes 262144
  34.3 1.6 %copy.13 = f32[16,16,128]{2,1,0:T(8,128)} copy(f32[16,16,128]{2,1,0:T(8,128)} %get-tuple-element.7) | data formatting | bytes 262144
  35.9 0.0 copy-done
  35.9 0.7 %copy.14 = f32[3,16,16,128]{3,2,1,0:T(8,128)} copy(f32[3,16,16,128]{3,2,1,0:T(8,128)S(1)} %copy-done) | data formatting | bytes 786432
Async XLA Ops:
  32.7 3.2 %copy-start = (f32[3,16,16,128]{3,2,1,0:T(8,128)S(1)}, f32[3,16,16,128]{3,2,1,0:T(8,128)}, u32[]{:S(2)}) copy-start(f32[3,16,16,128]{3,2,1,0:T(8,128)} %get-tuple-element.8) | copy-start | bytes 1179652

commit v4 on v3

v4 whole, which is shorter than its diff:
```python
import functools

import jax
import jax.numpy as jnp
from jax import lax
from jax.experimental import pallas as pl
from jax.experimental.pallas import tpu as pltpu
from jax.sharding import PartitionSpec as P

ITERS = 4
MOMENTS = 2 * ITERS
MESH = pl.DeviceIdType.MESH
UNROLL = 4
VMEM_LIMIT = 62 * 1024 * 1024


def coefficients(mu):
    def norm(c):
        total = None
        for i in range(len(c)):
            for j in range(i, len(c)):
                term = c[i] * c[j] * mu[i + j]
                term = term if i == j else term + term
                total = term if total is None else total + term
        return total

    def curved(c):
        total = None
        for i in range(len(c)):
            for j in range(i, len(c)):
                term = c[i] * c[j] * (mu[i + j] - mu[i + j + 1])
                term = term if i == j else term + term
                total = term if total is None else total + term
        return total

    one = jnp.ones_like(mu[0])
    scaled, direction, answer = [one], [one], []
    norm_now = mu[0]
    for step in range(ITERS):
        alpha = norm_now / curved(direction)
        answer = [a + alpha * d for a, d in zip(answer, direction)] + [alpha * direction[-1]]
        if step + 1 < ITERS:
            image = [direction[0]]
            image += [b - a for a, b in zip(direction[:-1], direction[1:])]
            image += [-direction[-1]]
            scaled = [s - alpha * q for s, q in zip(scaled, image)] + [-alpha * image[-1]]
            fresh = norm(scaled)
            beta = fresh / norm_now
            direction = [s + beta * d for s, d in zip(scaled, direction)] + [scaled[-1]]
            norm_now = fresh
    return answer


def kernel(
    nx, ny,
    levels, mask_in, elec_in, leak_in, src_in, wgt_in,
    pot_out, adj_out, sens_out,
    mask, elec, leak, rhs, in_sem,
    cx, coef, coef_y_send, coef_y, coef_send, coef_recv,
    rim_x, rim_y, rim_y_send, rim_send, rim_recv,
    field, y_send, y_halo, corner_send, corner, halo_send, halo_recv,
    part, gathered, part_send, part_recv,
    answer, rims, sens, out_sem,
):
    bx, by_rows, nz = leak.shape
    ix, iy = lax.axis_index("gx"), lax.axis_index("gy")
    devices = nx * ny
    rank = ix * ny + iy
    has_x = (ix > 0, ix < nx - 1)
    has_y = (iy > 0, iy < ny - 1)
    to_x = (lax.rem(ix + nx - 1, nx), lax.rem(ix + 1, nx))
    to_y = (lax.rem(iy + ny - 1, ny), lax.rem(iy + 1, ny))
    edge_x, edge_y = (0, bx - 1), (0, by_rows - 1)

    loads = [
        pltpu.make_async_copy(mask_in, mask, in_sem.at[0]),
        pltpu.make_async_copy(elec_in, elec, in_sem.at[1]),
        pltpu.make_async_copy(leak_in, leak, in_sem.at[2]),
        pltpu.make_async_copy(src_in, rhs.at[0], in_sem.at[3]),
        pltpu.make_async_copy(wgt_in, rhs.at[1], in_sem.at[4]),
    ]
    for load in loads:
        load.start()

    def other(k):
        at = lax.rem(rank + k, devices)
        return {"gx": lax.div(at, ny), "gy": lax.rem(at, ny)}

    def each_other(act):
        def step(k, carry):
            act(k)
            return carry

        lax.fori_loop(1, devices, step, 0)

    barrier = pltpu.get_barrier_semaphore()
    each_other(lambda k: pl.semaphore_signal(barrier, inc=1, device_id=other(k), device_id_type=MESH))
    pl.semaphore_wait(barrier, devices - 1)

    loads[0].wait()
    row = lax.broadcasted_iota(jnp.int32, (by_rows, nz), 0)
    lane = lax.broadcasted_iota(jnp.int32, (by_rows, nz), 1)
    row_x = lax.broadcasted_iota(jnp.int32, (bx, nz), 0)
    rim_y_send[...] = mask[1, :, by_rows - 1 : by_rows, :]
    rim_copy_x = pltpu.make_async_remote_copy(
        mask.at[0, bx - 1], rim_x, rim_send.at[0], rim_recv.at[0],
        device_id={"gx": to_x[1]}, device_id_type=MESH,
    )
    rim_copy_y = pltpu.make_async_remote_copy(
        rim_y_send, rim_y, rim_send.at[1], rim_recv.at[1],
        device_id={"gy": to_y[1]}, device_id_type=MESH,
    )
    pl.when(has_x[1])(rim_copy_x.start)
    pl.when(has_y[1])(rim_copy_y.start)

    @pl.when(jnp.logical_not(has_x[0]))
    def _():
        rim_x[...] = jnp.zeros_like(rim_x)

    @pl.when(jnp.logical_not(has_y[0]))
    def _():
        rim_y[...] = jnp.zeros_like(rim_y)

    for side in range(2):

        @pl.when(jnp.logical_not(has_x[side]))
        def _(side=side):
            for at in (0, 1) if side == 0 else (bx + 2, bx + 3):
                for k in range(ITERS):
                    for f in range(2):
                        field[k, f, at] = jnp.zeros((by_rows, nz), jnp.float32)
            for c in range(7):
                coef[c, 0 if side == 0 else bx + 1] = jnp.zeros((by_rows, nz), jnp.float32)

        @pl.when(jnp.logical_not(has_y[side]))
        def _(side=side):
            coef_y[side] = jnp.zeros_like(coef_y[side])
            for k in range(ITERS):
                y_halo[k, side] = jnp.zeros_like(y_halo[k, side])

    for c in range(4):

        @pl.when(jnp.logical_not(jnp.logical_and(has_x[c // 2], has_y[c % 2])))
        def _(c=c):
            for e in range(ITERS // 2):
                corner[e, c] = jnp.zeros_like(corner[e, c])

    def conductance(bits, d):
        return jnp.where(bits == 1, levels[1, d], levels[0, d])

    x_low = has_x[0].astype(jnp.float32)
    x_high = has_x[1].astype(jnp.float32)
    y_low = has_y[0].astype(jnp.float32)
    y_high = has_y[1].astype(jnp.float32)
    not_last_row = jnp.where(row < by_rows - 1, 1.0, y_high)
    for load in loads[1:]:
        load.wait()
    square = (by_rows, by_rows)
    eye = lax.broadcasted_iota(jnp.int32, square, 0) == lax.broadcasted_iota(jnp.int32, square, 1)

    def column(which, x):
        line = elec[which, pl.ds(x, 1), :].astype(jnp.float32)
        return jnp.sum(jnp.where(eye, line, 0.0), axis=1, keepdims=True)

    def set_up(x, carry):
        here = conductance(mask[0, x], 0) * jnp.where(x < bx - 1, 1.0, x_high)
        cx[x + 1] = here
        here_y = conductance(mask[1, x], 1) * not_last_row
        coef[2, x + 1] = here_y
        here_z = jnp.where(lane < nz - 1, conductance(mask[2, x], 2), 0.0)
        coef[4, x + 1] = here_z
        back_z = pltpu.roll(here_z, 1, 1)
        coef[5, x + 1] = back_z
        first = jnp.where(lane == 0, column(0, x), 0.0)
        last = jnp.where(lane == nz - 1, column(1, x), 0.0)
        rhs[0, x] = rhs[0, x] + first
        rhs[1, x] = rhs[1, x] + last
        leak[x] = leak[x] + first + last + here + here_y + here_z + back_z
        return carry

    lax.fori_loop(0, bx, set_up, 0, unroll=UNROLL)
    pl.when(has_x[0])(rim_copy_x.wait_recv)
    pl.when(has_y[0])(rim_copy_y.wait_recv)
    cx[0] = conductance(rim_x[...], 0) * x_low

    def halos(k):
        e = k // 2
        copies = []
        for side in range(2):
            mine, theirs = ((2, bx + 2), (bx, 0))[side]
            copies.append((has_x[side], has_x[1 - side], pltpu.make_async_remote_copy(
                field.at[k, :, pl.ds(mine, 2)], field.at[k, :, pl.ds(theirs, 2)],
                halo_send.at[e, side], halo_recv.at[e, side],
                device_id={"gx": to_x[side]}, device_id_type=MESH)))
            copies.append((has_y[side], has_y[1 - side], pltpu.make_async_remote_copy(
                y_send.at[e, side], y_halo.at[k, 1 - side],
                halo_send.at[e, 2 + side], halo_recv.at[e, 2 + side],
                device_id={"gy": to_y[side]}, device_id_type=MESH)))
        for c in range(4):
            a, b = c // 2, c % 2
            copies.append((
                jnp.logical_and(has_x[a], has_y[b]), jnp.logical_and(has_x[1 - a], has_y[1 - b]),
                pltpu.make_async_remote_copy(
                    corner_send.at[e, c], corner.at[e, 3 - c], halo_send.at[e, 4 + c], halo_recv.at[e, 4 + c],
                    device_id={"gx": to_x[a], "gy": to_y[b]}, device_id_type=MESH)))
        return copies

    def coef_copies():
        copies = []
        for side in range(2):
            mine, theirs = ((1, bx + 1), (bx, 0))[side]
            copies.append((has_x[side], has_x[1 - side], pltpu.make_async_remote_copy(
                coef.at[:, mine], coef.at[:, theirs], coef_send.at[side], coef_recv.at[side],
                device_id={"gx": to_x[side]}, device_id_type=MESH)))
            copies.append((has_y[side], has_y[1 - side], pltpu.make_async_remote_copy(
                coef_y_send.at[side], coef_y.at[1 - side], coef_send.at[2 + side], coef_recv.at[2 + side],
                device_id={"gy": to_y[side]}, device_id_type=MESH)))
        return copies

    def start(copies):
        for sends, _, copy in copies:
            pl.when(sends)(copy.start)

    def arrive(copies):
        for _, receives, copy in copies:
            pl.when(receives)(copy.wait_recv)

    def put(k, f, x, value):
        field[k, f, x + 2] = value
        if k % 2 == 0:
            for side in range(2):
                for deep in range(2):
                    at = deep if side == 0 else by_rows - 1 - deep
                    y_send[k // 2, side, f, deep, pl.ds(x, 1), :] = value[at : at + 1]

    def send(k):
        for c in range(4):
            at = edge_x[c // 2]
            for f in range(2):
                corner_send[k // 2, c, f] = y_send[k // 2, c % 2, f, 0, at : at + 1, :]
        start(halos(k))

    def fold(value):
        total = value[0:8]
        for at in range(8, by_rows, 8):
            total = total + value[at : at + 8]
        return total

    nought = jnp.zeros((8, nz), jnp.float32)

    def begin(x, sums):
        here_x, back_x, here_y = cx[x + 1], cx[x], coef[2, x + 1]
        back_y = jnp.where(row == 0, conductance(rim_y[x], 1) * y_low, pltpu.roll(here_y, 1, 0))
        scale = 1.0 / (leak[x] + back_x + back_y)
        coef[0, x + 1] = here_x
        coef[1, x + 1] = back_x
        coef[3, x + 1] = back_y
        coef[6, x + 1] = scale
        for c, value in enumerate((here_x, back_x, here_y, back_y, coef[4, x + 1], coef[5, x + 1], scale)):
            for side in range(2):
                at = edge_y[side]
                coef_y_send[side, c, pl.ds(x, 1), :] = value[at : at + 1]
        out = []
        for f in range(2):
            value = rhs[f, x] * scale
            put(0, f, x, value)
            out.append(sums[f] + fold(rhs[f, x] * value))
        return tuple(out)

    moments = [lax.fori_loop(0, bx, begin, (nought, nought), unroll=UNROLL)]

    def stencil(here, dn_x, up_x, dn_y, up_y, c):
        total = c[0] * up_x + c[1] * dn_x
        total = total + (c[2] * up_y + c[3] * dn_y)
        return total + (c[4] * pltpu.roll(here, nz - 1, 1) + c[5] * pltpu.roll(here, 1, 1))

    def beside(k, f, x, low, high):
        here = field[k, f, x + 2]
        up_y = jnp.where(row == by_rows - 1, high, pltpu.roll(here, by_rows - 1, 0))
        dn_y = jnp.where(row == 0, low, pltpu.roll(here, 1, 0))
        c = [coef[i, x + 1] for i in range(6)]
        return here, stencil(here, field[k, f, x + 1], field[k, f, x + 3], dn_y, up_y, c)

    def ghosts(k):
        e = k // 2
        for f in range(2):
            for side in range(2):
                x = (-1, bx)[side]
                _, total = beside(k, f, x, corner[e, 2 * side, f], corner[e, 2 * side + 1, f])
                field[k + 1, f, x + 2] = total * coef[6, x + 1]
                here, outer, own = y_halo[k, side, f, 0], y_halo[k, side, f, 1], y_send[e, side, f, 0]
                dn_x = jnp.where(row_x == 0, corner[e, side, f], pltpu.roll(here, 1, 0))
                up_x = jnp.where(row_x == bx - 1, corner[e, 2 + side, f], pltpu.roll(here, bx - 1, 0))
                dn_y, up_y = (outer, own) if side == 0 else (own, outer)
                total = stencil(here, dn_x, up_x, dn_y, up_y, [coef_y[side, i] for i in range(6)])
                y_halo[k + 1, side, f, 0] = total * coef_y[side, 6]

    for k in range(ITERS):
        if k % 2 == 0:
            send(k)
            if k == 0:
                start(coef_copies())
            arrive(halos(k))

        def advance(x, sums, k=k):
            out = []
            for f in range(2):
                low, high = [y_halo[k, side, f, 0, pl.ds(x, 1), :] for side in range(2)]
                here, total = beside(k, f, x, low, high)
                out.append(sums[len(out)] + fold(here * total))
                if k + 1 < ITERS:
                    value = total * coef[6, x + 1]
                    put(k + 1, f, x, value)
                    out.append(sums[len(out)] + fold(value * total))
            return tuple(out)

        count = 4 if k + 1 < ITERS else 2
        sums = lax.fori_loop(0, bx, advance, (nought,) * count, unroll=UNROLL)
        if k + 1 < ITERS:
            moments += [(sums[0], sums[2]), (sums[1], sums[3])]
        else:
            moments += [(sums[0], sums[1])]
        if k % 2 == 0:
            if k == 0:
                arrive(coef_copies())
            ghosts(k)

    rows = 2 * MOMENTS
    pick = lax.broadcasted_iota(jnp.int32, (rows, nz), 0) == lax.broadcasted_iota(jnp.int32, (rows, nz), 1)
    lines = [jnp.sum(value, axis=0, keepdims=True) for pair in moments for value in pair]
    each = jnp.sum(jnp.concatenate(lines, axis=0), axis=1, keepdims=True)
    message = jnp.sum(jnp.where(pick, each, 0.0), axis=0, keepdims=True)

    part[...] = message
    gathered[rank] = message
    each_other(lambda k: pltpu.make_async_remote_copy(
        part, gathered.at[rank], part_send, part_recv, device_id=other(k), device_id_type=MESH,
    ).start())
    others = gathered.at[pl.ds(0, devices - 1)]
    pltpu.make_async_copy(others, others, part_recv).wait()
    message = jnp.sum(gathered[...], axis=0)

    square = jnp.sum(jnp.where(pick, message, 0.0), axis=1, keepdims=True)
    square = jnp.broadcast_to(square, (rows, nz))
    weights = coefficients([square[2 * k : 2 * k + 2] for k in range(MOMENTS)])
    weights = [[jnp.broadcast_to(w[f : f + 1], (by_rows, nz)) for w in weights] for f in range(2)]

    def combine(x, carry):
        for f in range(2):
            total = weights[f][0] * field[0, f, x + 2]
            for k in range(1, ITERS):
                total = total + weights[f][k] * field[k, f, x + 2]
            answer[f, x] = total
        return carry

    lax.fori_loop(0, bx + 1, combine, 0, unroll=UNROLL)
    for f in range(2):
        rim = weights[f][0] * y_halo[0, 1, f, 0]
        for k in range(1, ITERS):
            rim = rim + weights[f][k] * y_halo[k, 1, f, 0]
        rims[f] = rim
    stores = [
        pltpu.make_async_copy(answer.at[0, pl.ds(0, bx)], pot_out, out_sem.at[0]),
        pltpu.make_async_copy(answer.at[1, pl.ds(0, bx)], adj_out, out_sem.at[1]),
        pltpu.make_async_copy(sens, sens_out, out_sem.at[2]),
    ]
    stores[0].start()
    stores[1].start()

    def differences(x, carry):
        gaps = []
        for f in range(2):
            here = answer[f, x]
            up_y = jnp.where(row == by_rows - 1, rims[f, pl.ds(x, 1), :], pltpu.roll(here, by_rows - 1, 0))
            gaps.append((here - answer[f, x + 1], here - up_y, here - pltpu.roll(here, nz - 1, 1)))
        sens[0, x] = -gaps[1][0] * gaps[0][0] * jnp.where(x < bx - 1, 1.0, x_high)
        sens[1, x] = -gaps[1][1] * gaps[0][1] * not_last_row
        sens[2, x] = jnp.where(lane < nz - 1, -gaps[1][2] * gaps[0][2], 0.0)
        return carry

    lax.fori_loop(0, bx, differences, 0, unroll=UNROLL)
    stores[2].start()

    pl.when(has_x[1])(rim_copy_x.wait_send)
    pl.when(has_y[1])(rim_copy_y.wait_send)
    for sends, _, copy in coef_copies() + halos(0) + halos(2):
        pl.when(sends)(copy.wait_send)
    pltpu.make_async_copy(others, others, part_send).wait()
    for store in stores:
        store.wait()


def body(nx, ny, bond_mask, levels, electrode, leakage, source, weight):
    bx, by, nz = leakage.shape
    f32, i32 = jnp.float32, jnp.int32
    vmem, dma = pltpu.VMEM, pltpu.SemaphoreType.DMA
    block = (bx, by, nz)
    hbm = pl.BlockSpec(memory_space=pltpu.HBM)
    return pl.pallas_call(
        functools.partial(kernel, nx, ny),
        out_shape=(
            jax.ShapeDtypeStruct(block, f32),
            jax.ShapeDtypeStruct(block, f32),
            jax.ShapeDtypeStruct((3,) + block, f32),
        ),
        in_specs=[pl.BlockSpec(memory_space=pltpu.SMEM)] + [hbm] * 5,
        out_specs=[hbm] * 3,
        scratch_shapes=[
            vmem((3,) + block, i32), vmem((2, bx, by), i32), vmem(block, f32), vmem((2,) + block, f32), dma((5,)),
            vmem((bx + 1, by, nz), f32), vmem((7, bx + 2, by, nz), f32),
            vmem((2, 7, bx, nz), f32), vmem((2, 7, bx, nz), f32), dma((4,)), dma((4,)),
            vmem((by, nz), i32), vmem((bx, 1, nz), i32), vmem((bx, 1, nz), i32), dma((2,)), dma((2,)),
            vmem((ITERS, 2, bx + 4, by, nz), f32),
            vmem((ITERS // 2, 2, 2, 2, bx, nz), f32), vmem((ITERS, 2, 2, 2, bx, nz), f32),
            vmem((ITERS // 2, 4, 2, 1, nz), f32), vmem((ITERS // 2, 4, 2, 1, nz), f32),
            dma((ITERS // 2, 8)), dma((ITERS // 2, 8)),
            vmem((1, nz), f32), vmem((nx * ny, 1, nz), f32), dma, dma,
            vmem((2, bx + 1, by, nz), f32), vmem((2, bx, nz), f32), vmem((3,) + block, f32), dma((3,)),
        ],
        compiler_params=pltpu.CompilerParams(
            collective_id=0, has_side_effects=True, vmem_limit_bytes=VMEM_LIMIT
        ),
    )(levels, bond_mask, electrode, leakage, source, weight)


def solution(mesh):
    return jax.shard_map(
        functools.partial(body, mesh.shape["gx"], mesh.shape["gy"]),
        mesh=mesh,
        in_specs=(
            P(None, "gx", "gy", None),
            P(),
            P(None, "gx", "gy"),
            P("gx", "gy", None),
            P("gx", "gy", None),
            P("gx", "gy", None),
        ),
        out_specs=(P("gx", "gy", None), P("gx", "gy", None), P(None, "gx", "gy", None)),
        check_vma=False,
    )
```

time: 36.8 us -> 30.8 us (0.84)
  Pallas kernels: 32.1 us -> 26 us
    pallas_call x1, Pallas kernels: 32.1 us -> 26 us  [body(): pl.pallas_call(functools.partial(kernel, nx, ny), out_shape=(jax.ShapeDty...]
where the time goes in v4:
time: 30.8 us; the launch traced here: 30.6 us
  Pallas kernels  26 us (84%)
  local copies, waits for them, and re-layouts  3.93 us (13%)
  between operations  0.65 us (2%)
    pallas_call x1, Pallas kernels, body(): pl.pallas_call(functools.partial(kernel, nx, ny), out_shape=(jax.ShapeDty...  26 us
    unnamed x5, local copies, waits for them, and re-layouts  3.93 us

profile of v4, /device:TPU:0, one launch (start us, length us, event | category | flops | bytes accessed | tf_op | source)
XLA Modules:
  0.0 30.6 jit_solution(1329064936018127046)
XLA Ops:
  0.6 26.0 %shard_map.85 = (f32[16,16,128]{2,1,0:T(8,128)}, f32[16,16,128]{2,1,0:T(8,128)}, f32[3,16,16,128]{3,2,1,0:T(8,128)}) custom-call(f32[2,3]{1,0:T(2,128)} %levels.1, s32[3,16,16,128]{3,2,1,0:T(8,128)} %mask_in.1, s32[2,16,16]{2,1,0:T(8,128)} %elec_in.1, f32[16,16,128]{2,1,0:T(8,128)} %leak_in.1, f32[16,16,128]{2,1,0:T(8,128)} %src_in.1, f32[16,16,128]{2,1,0:T(8,128)} %wgt_in.1), custom_call_target="tpu_custom_call" | custom-call | tf_op jit(solution)/shard_map/pallas_call | solution.py:399
  26.6 0.0 copy-start
  26.7 1.6 %copy.12 = f32[16,16,128]{2,1,0:T(8,128)} copy(f32[16,16,128]{2,1,0:T(8,128)} %get-tuple-element.6) | data formatting | bytes 262144
  28.3 1.6 %copy.13 = f32[16,16,128]{2,1,0:T(8,128)} copy(f32[16,16,128]{2,1,0:T(8,128)} %get-tuple-element.7) | data formatting | bytes 262144
  29.8 0.0 copy-done
  29.8 0.7 %copy.14 = f32[3,16,16,128]{3,2,1,0:T(8,128)} copy(f32[3,16,16,128]{3,2,1,0:T(8,128)S(1)} %copy-done) | data formatting | bytes 786432
Async XLA Ops:
  26.6 3.2 %copy-start = (f32[3,16,16,128]{3,2,1,0:T(8,128)S(1)}, f32[3,16,16,128]{3,2,1,0:T(8,128)}, u32[]{:S(2)}) copy-start(f32[3,16,16,128]{3,2,1,0:T(8,128)} %get-tuple-element.8) | copy-start | bytes 1179652

commit v5 on v4

--- a/solution.py
+++ b/solution.py
@@ -15,36 +15,30 @@
 
 
 def coefficients(mu):
-    def norm(c):
-        total = None
-        for i in range(len(c)):
-            for j in range(i, len(c)):
-                term = c[i] * c[j] * mu[i + j]
-                term = term if i == j else term + term
-                total = term if total is None else total + term
-        return total
-
-    def curved(c):
-        total = None
-        for i in range(len(c)):
-            for j in range(i, len(c)):
-                term = c[i] * c[j] * (mu[i + j] - mu[i + j + 1])
-                term = term if i == j else term + term
-                total = term if total is None else total + term
-        return total
-
+    def tree(terms):
+        while len(terms) > 1:
+            terms = [sum(terms[i : i + 2][1:], terms[i]) for i in range(0, len(terms), 2)]
+        return terms[0]
+
+    def quadratic(c, m):
+        return tree([
+            tree([c[i] * c[k - i] for i in range(max(0, k - len(c) + 1), min(k + 1, len(c)))]) * m[k]
+            for k in range(2 * len(c) - 1)
+        ])
+
+    slope = [a - b for a, b in zip(mu[:-1], mu[1:])]
     one = jnp.ones_like(mu[0])
     scaled, direction, answer = [one], [one], []
     norm_now = mu[0]
     for step in range(ITERS):
-        alpha = norm_now / curved(direction)
+        alpha = norm_now / quadratic(direction, slope)
         answer = [a + alpha * d for a, d in zip(answer, direction)] + [alpha * direction[-1]]
         if step + 1 < ITERS:
             image = [direction[0]]
             image += [b - a for a, b in zip(direction[:-1], direction[1:])]
             image += [-direction[-1]]
             scaled = [s - alpha * q for s, q in zip(scaled, image)] + [-alpha * image[-1]]
-            fresh = norm(scaled)
+            fresh = quadratic(scaled, mu)
             beta = fresh / norm_now
             direction = [s + beta * d for s, d in zip(scaled, direction)] + [scaled[-1]]
             norm_now = fresh
@@ -54,13 +48,13 @@
 def kernel(
     nx, ny,
     levels, mask_in, elec_in, leak_in, src_in, wgt_in,
-    pot_out, adj_out, sens_out,
+    answer_out, rims_out,
     mask, elec, leak, rhs, in_sem,
     cx, coef, coef_y_send, coef_y, coef_send, coef_recv,
     rim_x, rim_y, rim_y_send, rim_send, rim_recv,
     field, y_send, y_halo, corner_send, corner, halo_send, halo_recv,
     part, gathered, part_send, part_recv,
-    answer, rims, sens, out_sem,
+    answer, rims, out_sem,
 ):
     bx, by_rows, nz = leak.shape
     ix, iy = lax.axis_index("gx"), lax.axis_index("gy")
@@ -256,10 +250,6 @@
         coef[1, x + 1] = back_x
         coef[3, x + 1] = back_y
         coef[6, x + 1] = scale
-        for c, value in enumerate((here_x, back_x, here_y, back_y, coef[4, x + 1], coef[5, x + 1], scale)):
-            for side in range(2):
-                at = edge_y[side]
-                coef_y_send[side, c, pl.ds(x, 1), :] = value[at : at + 1]
         out = []
         for f in range(2):
             value = rhs[f, x] * scale
@@ -268,6 +258,13 @@
         return tuple(out)
 
     moments = [lax.fori_loop(0, bx, begin, (nought, nought), unroll=UNROLL)]
+
+    def stage(x, carry):
+        for c in range(7):
+            for side in range(2):
+                at = edge_y[side]
+                coef_y_send[side, c, pl.ds(x, 1), :] = coef[c, x + 1, at : at + 1, :]
+        return carry
 
     def stencil(here, dn_x, up_x, dn_y, up_y, c):
         total = c[0] * up_x + c[1] * dn_x
@@ -299,6 +296,7 @@
         if k % 2 == 0:
             send(k)
             if k == 0:
+                lax.fori_loop(0, bx, stage, 0, unroll=UNROLL)
                 start(coef_copies())
             arrive(halos(k))
 
@@ -360,12 +358,42 @@
             rim = rim + weights[f][k] * y_halo[k, 1, f, 0]
         rims[f] = rim
     stores = [
+        pltpu.make_async_copy(answer, answer_out, out_sem.at[0]),
+        pltpu.make_async_copy(rims, rims_out, out_sem.at[1]),
+    ]
+    for store in stores:
+        store.start()
+    pl.when(has_x[1])(rim_copy_x.wait_send)
+    pl.when(has_y[1])(rim_copy_y.wait_send)
+    for sends, _, copy in coef_copies() + halos(0) + halos(2):
+        pl.when(sends)(copy.wait_send)
+    pltpu.make_async_copy(others, others, part_send).wait()
+    for store in stores:
+        store.wait()
+
+
+def finish(nx, ny, answer_in, rims_in, pot_out, adj_out, sens_out, answer, rims, sens, in_sem, out_sem):
+    bx, by_rows, nz = pot_out.shape
+    loads = [
+        pltpu.make_async_copy(answer_in, answer, in_sem.at[0]),
+        pltpu.make_async_copy(rims_in, rims, in_sem.at[1]),
+    ]
+    for load in loads:
+        load.start()
+    stores = [
         pltpu.make_async_copy(answer.at[0, pl.ds(0, bx)], pot_out, out_sem.at[0]),
         pltpu.make_async_copy(answer.at[1, pl.ds(0, bx)], adj_out, out_sem.at[1]),
         pltpu.make_async_copy(sens, sens_out, out_sem.at[2]),
     ]
+    loads[0].wait()
     stores[0].start()
     stores[1].start()
+    loads[1].wait()
+    row = lax.broadcasted_iota(jnp.int32, (by_rows, nz), 0)
+    lane = lax.broadcasted_iota(jnp.int32, (by_rows, nz), 1)
+    x_high = (lax.axis_index("gx") < nx - 1).astype(jnp.float32)
+    y_high = (lax.axis_index("gy") < ny - 1).astype(jnp.float32)
+    not_last_row = jnp.where(row < by_rows - 1, 1.0, y_high)
 
     def differences(x, carry):
         gaps = []
@@ -380,12 +408,6 @@
 
     lax.fori_loop(0, bx, differences, 0, unroll=UNROLL)
     stores[2].start()
-
-    pl.when(has_x[1])(rim_copy_x.wait_send)
-    pl.when(has_y[1])(rim_copy_y.wait_send)
-    for sends, _, copy in coef_copies() + halos(0) + halos(2):
-        pl.when(sends)(copy.wait_send)
-    pltpu.make_async_copy(others, others, part_send).wait()
     for store in stores:
         store.wait()
 
@@ -396,15 +418,14 @@
     vmem, dma = pltpu.VMEM, pltpu.SemaphoreType.DMA
     block = (bx, by, nz)
     hbm = pl.BlockSpec(memory_space=pltpu.HBM)
-    return pl.pallas_call(
+    answer, rims = pl.pallas_call(
         functools.partial(kernel, nx, ny),
         out_shape=(
-            jax.ShapeDtypeStruct(block, f32),
-            jax.ShapeDtypeStruct(block, f32),
-            jax.ShapeDtypeStruct((3,) + block, f32),
+            jax.ShapeDtypeStruct((2, bx + 1, by, nz), f32),
+            jax.ShapeDtypeStruct((2, bx, nz), f32),
         ),
         in_specs=[pl.BlockSpec(memory_space=pltpu.SMEM)] + [hbm] * 5,
-        out_specs=[hbm] * 3,
+        out_specs=[hbm] * 2,
         scratch_shapes=[
             vmem((3,) + block, i32), vmem((2, bx, by), i32), vmem(block, f32), vmem((2,) + block, f32), dma((5,)),
             vmem((bx + 1, by, nz), f32), vmem((7, bx + 2, by, nz), f32),
@@ -415,12 +436,26 @@
             vmem((ITERS // 2, 4, 2, 1, nz), f32), vmem((ITERS // 2, 4, 2, 1, nz), f32),
             dma((ITERS // 2, 8)), dma((ITERS // 2, 8)),
             vmem((1, nz), f32), vmem((nx * ny, 1, nz), f32), dma, dma,
-            vmem((2, bx + 1, by, nz), f32), vmem((2, bx, nz), f32), vmem((3,) + block, f32), dma((3,)),
+            vmem((2, bx + 1, by, nz), f32), vmem((2, bx, nz), f32), dma((2,)),
         ],
         compiler_params=pltpu.CompilerParams(
             collective_id=0, has_side_effects=True, vmem_limit_bytes=VMEM_LIMIT
         ),
     )(levels, bond_mask, electrode, leakage, source, weight)
+    return pl.pallas_call(
+        functools.partial(finish, nx, ny),
+        out_shape=(
+            jax.ShapeDtypeStruct(block, f32),
+            jax.ShapeDtypeStruct(block, f32),
+            jax.ShapeDtypeStruct((3,) + block, f32),
+        ),
+        in_specs=[hbm] * 2,
+        out_specs=[hbm] * 3,
+        scratch_shapes=[
+            vmem((2, bx + 1, by, nz), f32), vmem((2, bx, nz), f32), vmem((3,) + block, f32), dma((2,)), dma((3,)),
+        ],
+        compiler_params=pltpu.CompilerParams(vmem_limit_bytes=VMEM_LIMIT),
+    )(answer, rims)
 
 
 def solution(mesh):

time: 30.8 us -> 28.4 us (0.922)
  local copies, waits for them, and re-layouts: 3.93 us -> 0 us
  Pallas kernels: 26 us -> 27.7 us
    unnamed x5 -> x0, local copies, waits for them, and re-layouts: 3.93 us -> none
    pallas_call x0 -> x1, Pallas kernels: none -> 2.1 us  [body(): pl.pallas_call(functools.partial(finish, nx, ny), out_shape=(jax.ShapeDty...]
    pallas_call x1, Pallas kernels: 26 us -> 25.6 us  [body(): pl.pallas_call(functools.partial(kernel, nx, ny), out_shape=(jax.ShapeDty...]
where the time goes in v5:
time: 28.4 us; the launch traced here: 28.3 us
  Pallas kernels  27.7 us (98%)
  between operations  0.64 us (2%)
    pallas_call x1, Pallas kernels, body(): pl.pallas_call(functools.partial(kernel, nx, ny), out_shape=(jax.ShapeDty...  25.6 us
    pallas_call x1, Pallas kernels, body(): pl.pallas_call(functools.partial(finish, nx, ny), out_shape=(jax.ShapeDty...  2.1 us

profile of v5, /device:TPU:0, one launch (start us, length us, event | category | flops | bytes accessed | tf_op | source)
XLA Modules:
  0.0 28.3 jit_solution(8398559228631256322)
XLA Ops:
  0.6 25.6 %shard_map.85 = (f32[2,17,16,128]{3,2,1,0:T(8,128)}, f32[2,16,128]{2,1,0:T(8,128)}) custom-call(f32[2,3]{1,0:T(2,128)} %levels.1, s32[3,16,16,128]{3,2,1,0:T(8,128)} %mask_in.1, s32[2,16,16]{2,1,0:T(8,128)} %elec_in.1, f32[16,16,128]{2,1,0:T(8,128)} %leak_in.1, f32[16,16,128]{2,1,0:T(8,128)} %src_in.1, f32[16,16,128]{2,1,0:T(8,128)} %wgt_in.1), custom_call_target="tpu_custom_call" | custom-call | tf_op jit(solution)/shard_map/pallas_call | solution.py:421
  26.2 2.1 %shard_map.86 = (f32[16,16,128]{2,1,0:T(8,128)}, f32[16,16,128]{2,1,0:T(8,128)}, f32[3,16,16,128]{3,2,1,0:T(8,128)}) custom-call(f32[2,17,16,128]{3,2,1,0:T(8,128)} %get-tuple-element.5.answer_in, f32[2,16,128]{2,1,0:T(8,128)} %get-tuple-element.6.rims_in), custom_call_target="tpu_custom_call" | custom-call | tf_op jit(solution)/shard_map/pallas_call | solution.py:445

commit v6 on v5

--- a/solution.py
+++ b/solution.py
@@ -62,8 +62,8 @@
     rank = ix * ny + iy
     has_x = (ix > 0, ix < nx - 1)
     has_y = (iy > 0, iy < ny - 1)
-    to_x = (lax.rem(ix + nx - 1, nx), lax.rem(ix + 1, nx))
-    to_y = (lax.rem(iy + ny - 1, ny), lax.rem(iy + 1, ny))
+    to_x = (jnp.maximum(ix - 1, 0), jnp.minimum(ix + 1, nx - 1))
+    to_y = (jnp.maximum(iy - 1, 0), jnp.minimum(iy + 1, ny - 1))
     edge_x, edge_y = (0, bx - 1), (0, by_rows - 1)
 
     loads = [
@@ -76,19 +76,23 @@
     for load in loads:
         load.start()
 
-    def other(k):
-        at = lax.rem(rank + k, devices)
-        return {"gx": lax.div(at, ny), "gy": lax.rem(at, ny)}
+    def ahead(at, count, size):
+        places = [at]
+        for _ in range(1, count):
+            later = places[-1] + 1
+            places.append(jnp.where(later == size, 0, later))
+        return places
+
+    all_x, all_y = ahead(ix, nx, nx), ahead(iy, ny, ny)
 
     def each_other(act):
-        def step(k, carry):
-            act(k)
-            return carry
-
-        lax.fori_loop(1, devices, step, 0)
+        for dx in range(nx):
+            for dy in range(ny):
+                if dx or dy:
+                    act({"gx": all_x[dx], "gy": all_y[dy]})
 
     barrier = pltpu.get_barrier_semaphore()
-    each_other(lambda k: pl.semaphore_signal(barrier, inc=1, device_id=other(k), device_id_type=MESH))
+    each_other(lambda to: pl.semaphore_signal(barrier, inc=1, device_id=to, device_id_type=MESH))
     pl.semaphore_wait(barrier, devices - 1)
 
     loads[0].wait()
@@ -313,7 +317,7 @@
             return tuple(out)
 
         count = 4 if k + 1 < ITERS else 2
-        sums = lax.fori_loop(0, bx, advance, (nought,) * count, unroll=UNROLL)
+        sums = lax.fori_loop(0, bx, advance, (nought,) * count, unroll=bx)
         if k + 1 < ITERS:
             moments += [(sums[0], sums[2]), (sums[1], sums[3])]
         else:
@@ -331,8 +335,8 @@
 
     part[...] = message
     gathered[rank] = message
-    each_other(lambda k: pltpu.make_async_remote_copy(
-        part, gathered.at[rank], part_send, part_recv, device_id=other(k), device_id_type=MESH,
+    each_other(lambda to: pltpu.make_async_remote_copy(
+        part, gathered.at[rank], part_send, part_recv, device_id=to, device_id_type=MESH,
     ).start())
     others = gathered.at[pl.ds(0, devices - 1)]
     pltpu.make_async_copy(others, others, part_recv).wait()

time: 28.4 us -> 27.3 us (0.961)
  Pallas kernels: 27.7 us -> 26.5 us
    pallas_call x1, Pallas kernels: 25.6 us -> 24.4 us  [body(): pl.pallas_call(functools.partial(kernel, nx, ny), out_shape=(jax.ShapeDty...]
where the time goes in v6:
time: 27.3 us; the launch traced here: 27.1 us
  Pallas kernels  26.5 us (97%)
  between operations  0.64 us (2%)
    pallas_call x1, Pallas kernels, body(): pl.pallas_call(functools.partial(kernel, nx, ny), out_shape=(jax.ShapeDty...  24.4 us
    pallas_call x1, Pallas kernels, body(): pl.pallas_call(functools.partial(finish, nx, ny), out_shape=(jax.ShapeDty...  2.1 us

profile of v6, /device:TPU:0, one launch (start us, length us, event | category | flops | bytes accessed | tf_op | source)
XLA Modules:
  0.0 27.1 jit_solution(2397950760363102792)
XLA Ops:
  0.6 24.4 %shard_map.85 = (f32[2,17,16,128]{3,2,1,0:T(8,128)}, f32[2,16,128]{2,1,0:T(8,128)}) custom-call(f32[2,3]{1,0:T(2,128)} %levels.1, s32[3,16,16,128]{3,2,1,0:T(8,128)} %mask_in.1, s32[2,16,16]{2,1,0:T(8,128)} %elec_in.1, f32[16,16,128]{2,1,0:T(8,128)} %leak_in.1, f32[16,16,128]{2,1,0:T(8,128)} %src_in.1, f32[16,16,128]{2,1,0:T(8,128)} %wgt_in.1), custom_call_target="tpu_custom_call" | custom-call | tf_op jit(solution)/shard_map/pallas_call | solution.py:425
  25.0 2.1 %shard_map.86 = (f32[16,16,128]{2,1,0:T(8,128)}, f32[16,16,128]{2,1,0:T(8,128)}, f32[3,16,16,128]{3,2,1,0:T(8,128)}) custom-call(f32[2,17,16,128]{3,2,1,0:T(8,128)} %get-tuple-element.5.answer_in, f32[2,16,128]{2,1,0:T(8,128)} %get-tuple-element.6.rims_in), custom_call_target="tpu_custom_call" | custom-call | tf_op jit(solution)/shard_map/pallas_call | solution.py:449

commit v7 on v6

--- a/solution.py
+++ b/solution.py
@@ -53,7 +53,7 @@
     cx, coef, coef_y_send, coef_y, coef_send, coef_recv,
     rim_x, rim_y, rim_y_send, rim_send, rim_recv,
     field, y_send, y_halo, corner_send, corner, halo_send, halo_recv,
-    part, gathered, part_send, part_recv,
+    inner, part, gathered, part_send, part_recv,
     answer, rims, out_sem,
 ):
     bx, by_rows, nz = leak.shape
@@ -261,7 +261,7 @@
             out.append(sums[f] + fold(rhs[f, x] * value))
         return tuple(out)
 
-    moments = [lax.fori_loop(0, bx, begin, (nought, nought), unroll=UNROLL)]
+    moments = [lax.fori_loop(0, bx, begin, (nought, nought), unroll=bx)]
 
     def stage(x, carry):
         for c in range(7):
@@ -296,28 +296,57 @@
                 total = stencil(here, dn_x, up_x, dn_y, up_y, [coef_y[side, i] for i in range(6)])
                 y_halo[k + 1, side, f, 0] = total * coef_y[side, 6]
 
+    def within(k):
+        for x in range(bx):
+            c = [coef[i, x + 1] for i in range(6)]
+            for f in range(2):
+                here = field[k, f, x + 2]
+                up_y = jnp.where(row == by_rows - 1, 0.0, pltpu.roll(here, by_rows - 1, 0))
+                dn_y = jnp.where(row == 0, 0.0, pltpu.roll(here, 1, 0))
+                total = c[2] * up_y + c[3] * dn_y
+                total = total + (c[4] * pltpu.roll(here, nz - 1, 1) + c[5] * pltpu.roll(here, 1, 1))
+                if x > 0:
+                    total = total + c[1] * field[k, f, x + 1]
+                if x < bx - 1:
+                    total = total + c[0] * field[k, f, x + 3]
+                inner[f, x] = total
+
+    def completed(k, f, x):
+        total = inner[f, x]
+        if x == 0:
+            total = total + coef[1, 1] * field[k, f, 1]
+        if x == bx - 1:
+            total = total + coef[0, bx] * field[k, f, bx + 2]
+        low, high = [y_halo[k, side, f, 0, x : x + 1, :] for side in range(2)]
+        total = total + jnp.where(row == 0, coef[3, x + 1] * low, 0.0)
+        total = total + jnp.where(row == by_rows - 1, coef[2, x + 1] * high, 0.0)
+        return field[k, f, x + 2], total
+
     for k in range(ITERS):
         if k % 2 == 0:
             send(k)
             if k == 0:
+                start(coef_copies()[0::2])
                 lax.fori_loop(0, bx, stage, 0, unroll=UNROLL)
-                start(coef_copies())
+                start(coef_copies()[1::2])
+            within(k)
             arrive(halos(k))
-
-        def advance(x, sums, k=k):
-            out = []
+        sums = [nought] * (4 if k + 1 < ITERS else 2)
+        for x in range(bx):
+            at = 0
             for f in range(2):
-                low, high = [y_halo[k, side, f, 0, pl.ds(x, 1), :] for side in range(2)]
-                here, total = beside(k, f, x, low, high)
-                out.append(sums[len(out)] + fold(here * total))
+                if k % 2 == 0:
+                    here, total = completed(k, f, x)
+                else:
+                    low, high = [y_halo[k, side, f, 0, x : x + 1, :] for side in range(2)]
+                    here, total = beside(k, f, x, low, high)
+                sums[at] = sums[at] + fold(here * total)
+                at += 1
                 if k + 1 < ITERS:
                     value = total * coef[6, x + 1]
                     put(k + 1, f, x, value)
-                    out.append(sums[len(out)] + fold(value * total))
-            return tuple(out)
-
-        count = 4 if k + 1 < ITERS else 2
-        sums = lax.fori_loop(0, bx, advance, (nought,) * count, unroll=bx)
+                    sums[at] = sums[at] + fold(value * total)
+                    at += 1
         if k + 1 < ITERS:
             moments += [(sums[0], sums[2]), (sums[1], sums[3])]
         else:
@@ -355,7 +384,7 @@
             answer[f, x] = total
         return carry
 
-    lax.fori_loop(0, bx + 1, combine, 0, unroll=UNROLL)
+    lax.fori_loop(0, bx + 1, combine, 0, unroll=bx + 1)
     for f in range(2):
         rim = weights[f][0] * y_halo[0, 1, f, 0]
         for k in range(1, ITERS):
@@ -410,7 +439,7 @@
         sens[2, x] = jnp.where(lane < nz - 1, -gaps[1][2] * gaps[0][2], 0.0)
         return carry
 
-    lax.fori_loop(0, bx, differences, 0, unroll=UNROLL)
+    lax.fori_loop(0, bx, differences, 0, unroll=bx)
     stores[2].start()
     for store in stores:
         store.wait()
@@ -439,7 +468,7 @@
             vmem((ITERS // 2, 2, 2, 2, bx, nz), f32), vmem((ITERS, 2, 2, 2, bx, nz), f32),
             vmem((ITERS // 2, 4, 2, 1, nz), f32), vmem((ITERS // 2, 4, 2, 1, nz), f32),
             dma((ITERS // 2, 8)), dma((ITERS // 2, 8)),
-            vmem((1, nz), f32), vmem((nx * ny, 1, nz), f32), dma, dma,
+            vmem((2,) + block, f32), vmem((1, nz), f32), vmem((nx * ny, 1, nz), f32), dma, dma,
             vmem((2, bx + 1, by, nz), f32), vmem((2, bx, nz), f32), dma((2,)),
         ],
         compiler_params=pltpu.CompilerParams(

time: 27.3 us -> 26.9 us (0.985)
  Pallas kernels: 26.5 us -> 26.1 us
where the time goes in v7:
time: 26.9 us; the launch traced here: 26.7 us
  Pallas kernels  26.1 us (97%)
  between operations  0.64 us (2%)
    pallas_call x1, Pallas kernels, body(): pl.pallas_call(functools.partial(kernel, nx, ny), out_shape=(jax.ShapeDty...  24.2 us
    pallas_call x1, Pallas kernels, body(): pl.pallas_call(functools.partial(finish, nx, ny), out_shape=(jax.ShapeDty...  1.88 us

profile of v7, /device:TPU:0, one launch (start us, length us, event | category | flops | bytes accessed | tf_op | source)
XLA Modules:
  0.0 26.7 jit_solution(17144022140772670530)
XLA Ops:
  0.6 24.2 %shard_map.85 = (f32[2,17,16,128]{3,2,1,0:T(8,128)}, f32[2,16,128]{2,1,0:T(8,128)}) custom-call(f32[2,3]{1,0:T(2,128)} %levels.1, s32[3,16,16,128]{3,2,1,0:T(8,128)} %mask_in.1, s32[2,16,16]{2,1,0:T(8,128)} %elec_in.1, f32[16,16,128]{2,1,0:T(8,128)} %leak_in.1, f32[16,16,128]{2,1,0:T(8,128)} %src_in.1, f32[16,16,128]{2,1,0:T(8,128)} %wgt_in.1), custom_call_target="tpu_custom_call" | custom-call | tf_op jit(solution)/shard_map/pallas_call | solution.py:454
  24.9 1.9 %shard_map.86 = (f32[16,16,128]{2,1,0:T(8,128)}, f32[16,16,128]{2,1,0:T(8,128)}, f32[3,16,16,128]{3,2,1,0:T(8,128)}) custom-call(f32[2,17,16,128]{3,2,1,0:T(8,128)} %get-tuple-element.5.answer_in, f32[2,16,128]{2,1,0:T(8,128)} %get-tuple-element.6.rims_in), custom_call_target="tpu_custom_call" | custom-call | tf_op jit(solution)/shard_map/pallas_call | solution.py:478

commit v8 on v7

--- a/solution.py
+++ b/solution.py
@@ -50,7 +50,8 @@
     levels, mask_in, elec_in, leak_in, src_in, wgt_in,
     answer_out, rims_out,
     mask, elec, leak, rhs, in_sem,
-    cx, coef, coef_y_send, coef_y, coef_send, coef_recv,
+    cx, coef, factor_x_send, factor_x, factor_y_send, factor_y, factor_send, factor_recv,
+    own_x_send, own_x, own_y_send, own_y, own_send, own_recv,
     rim_x, rim_y, rim_y_send, rim_send, rim_recv,
     field, y_send, y_halo, corner_send, corner, halo_send, halo_recv,
     inner, part, gathered, part_send, part_recv,
@@ -123,16 +124,18 @@
 
         @pl.when(jnp.logical_not(has_x[side]))
         def _(side=side):
-            for at in (0, 1) if side == 0 else (bx + 2, bx + 3):
-                for k in range(ITERS):
-                    for f in range(2):
-                        field[k, f, at] = jnp.zeros((by_rows, nz), jnp.float32)
-            for c in range(7):
-                coef[c, 0 if side == 0 else bx + 1] = jnp.zeros((by_rows, nz), jnp.float32)
+            for k in range(ITERS):
+                for f in range(2):
+                    field[k, f, 1 if side == 0 else bx + 2] = jnp.zeros((by_rows, nz), jnp.float32)
+            factor_x[side] = jnp.zeros_like(factor_x[side])
+            for e in range(ITERS // 2):
+                own_x[e, side] = jnp.zeros_like(own_x[e, side])
 
         @pl.when(jnp.logical_not(has_y[side]))
         def _(side=side):
-            coef_y[side] = jnp.zeros_like(coef_y[side])
+            factor_y[side] = jnp.zeros_like(factor_y[side])
+            for e in range(ITERS // 2):
+                own_y[e, side] = jnp.zeros_like(own_y[e, side])
             for k in range(ITERS):
                 y_halo[k, side] = jnp.zeros_like(y_halo[k, side])
 
@@ -185,9 +188,9 @@
         e = k // 2
         copies = []
         for side in range(2):
-            mine, theirs = ((2, bx + 2), (bx, 0))[side]
+            mine, theirs = ((2, bx + 2), (bx + 1, 1))[side]
             copies.append((has_x[side], has_x[1 - side], pltpu.make_async_remote_copy(
-                field.at[k, :, pl.ds(mine, 2)], field.at[k, :, pl.ds(theirs, 2)],
+                field.at[k, :, mine], field.at[k, :, theirs],
                 halo_send.at[e, side], halo_recv.at[e, side],
                 device_id={"gx": to_x[side]}, device_id_type=MESH)))
             copies.append((has_y[side], has_y[1 - side], pltpu.make_async_remote_copy(
@@ -203,17 +206,25 @@
                     device_id={"gx": to_x[a], "gy": to_y[b]}, device_id_type=MESH)))
         return copies
 
-    def coef_copies():
+    def sided(x_from, x_to, y_from, y_to, sends, receives):
         copies = []
         for side in range(2):
-            mine, theirs = ((1, bx + 1), (bx, 0))[side]
             copies.append((has_x[side], has_x[1 - side], pltpu.make_async_remote_copy(
-                coef.at[:, mine], coef.at[:, theirs], coef_send.at[side], coef_recv.at[side],
+                x_from.at[side], x_to.at[1 - side], sends.at[side], receives.at[side],
                 device_id={"gx": to_x[side]}, device_id_type=MESH)))
             copies.append((has_y[side], has_y[1 - side], pltpu.make_async_remote_copy(
-                coef_y_send.at[side], coef_y.at[1 - side], coef_send.at[2 + side], coef_recv.at[2 + side],
+                y_from.at[side], y_to.at[1 - side], sends.at[2 + side], receives.at[2 + side],
                 device_id={"gy": to_y[side]}, device_id_type=MESH)))
         return copies
+
+    def factor_copies():
+        return sided(factor_x_send, factor_x, factor_y_send, factor_y, factor_send, factor_recv)
+
+    def own_copies(k):
+        e = k // 2
+        return sided(
+            own_x_send.at[e], own_x.at[e], own_y_send.at[e], own_y.at[e], own_send.at[e], own_recv.at[e]
+        )
 
     def start(copies):
         for sends, _, copy in copies:
@@ -227,15 +238,14 @@
         field[k, f, x + 2] = value
         if k % 2 == 0:
             for side in range(2):
-                for deep in range(2):
-                    at = deep if side == 0 else by_rows - 1 - deep
-                    y_send[k // 2, side, f, deep, pl.ds(x, 1), :] = value[at : at + 1]
+                at = edge_y[side]
+                y_send[k // 2, side, f, x : x + 1, :] = value[at : at + 1]
 
     def send(k):
         for c in range(4):
             at = edge_x[c // 2]
             for f in range(2):
-                corner_send[k // 2, c, f] = y_send[k // 2, c % 2, f, 0, at : at + 1, :]
+                corner_send[k // 2, c, f] = y_send[k // 2, c % 2, f, at : at + 1, :]
         start(halos(k))
 
     def fold(value):
@@ -246,7 +256,8 @@
 
     nought = jnp.zeros((8, nz), jnp.float32)
 
-    def begin(x, sums):
+    sums = [nought, nought]
+    for x in range(bx):
         here_x, back_x, here_y = cx[x + 1], cx[x], coef[2, x + 1]
         back_y = jnp.where(row == 0, conductance(rim_y[x], 1) * y_low, pltpu.roll(here_y, 1, 0))
         scale = 1.0 / (leak[x] + back_x + back_y)
@@ -254,21 +265,30 @@
         coef[1, x + 1] = back_x
         coef[3, x + 1] = back_y
         coef[6, x + 1] = scale
-        out = []
         for f in range(2):
             value = rhs[f, x] * scale
             put(0, f, x, value)
-            out.append(sums[f] + fold(rhs[f, x] * value))
-        return tuple(out)
-
-    moments = [lax.fori_loop(0, bx, begin, (nought, nought), unroll=bx)]
-
-    def stage(x, carry):
-        for c in range(7):
+            sums[f] = sums[f] + fold(rhs[f, x] * value)
+    moments = [tuple(sums)]
+
+    def factors():
+        for side in range(2):
+            factor_x_send[side, by_rows:, :] = jnp.zeros((8, nz), jnp.float32)
+            factor_y_send[side, bx:, :] = jnp.zeros((8, nz), jnp.float32)
+        for x in range(bx):
+            scale = coef[6, x + 1]
             for side in range(2):
                 at = edge_y[side]
-                coef_y_send[side, c, pl.ds(x, 1), :] = coef[c, x + 1, at : at + 1, :]
-        return carry
+                factor_y_send[side, x : x + 1, :] = (coef[(3, 2)[side], x + 1] * scale)[at : at + 1]
+        for side in range(2):
+            at = edge_x[side] + 1
+            factor_x_send[side, 0:by_rows, :] = coef[(1, 0)[side], at] * coef[6, at]
+        for side in range(2):
+            for end in range(2):
+                at = edge_x[side]
+                factor_x_send[side, by_rows + end : by_rows + end + 1, :] = factor_y_send[end, at : at + 1, :]
+                at = edge_y[side]
+                factor_y_send[side, bx + end : bx + end + 1, :] = factor_x_send[end, at : at + 1, :]
 
     def stencil(here, dn_x, up_x, dn_y, up_y, c):
         total = c[0] * up_x + c[1] * dn_x
@@ -284,17 +304,19 @@
 
     def ghosts(k):
         e = k // 2
-        for f in range(2):
-            for side in range(2):
-                x = (-1, bx)[side]
-                _, total = beside(k, f, x, corner[e, 2 * side, f], corner[e, 2 * side + 1, f])
-                field[k + 1, f, x + 2] = total * coef[6, x + 1]
-                here, outer, own = y_halo[k, side, f, 0], y_halo[k, side, f, 1], y_send[e, side, f, 0]
-                dn_x = jnp.where(row_x == 0, corner[e, side, f], pltpu.roll(here, 1, 0))
-                up_x = jnp.where(row_x == bx - 1, corner[e, 2 + side, f], pltpu.roll(here, bx - 1, 0))
-                dn_y, up_y = (outer, own) if side == 0 else (own, outer)
-                total = stencil(here, dn_x, up_x, dn_y, up_y, [coef_y[side, i] for i in range(6)])
-                y_halo[k + 1, side, f, 0] = total * coef_y[side, 6]
+        for side in range(2):
+            fx, fy = factor_x[side], factor_y[side]
+            for f in range(2):
+                total = own_x[e, side, f] + fx[0:by_rows] * field[k, f, edge_x[side] + 2]
+                total = total + jnp.where(row == 0, fx[by_rows : by_rows + 1] * corner[e, 2 * side, f], 0.0)
+                total = total + jnp.where(
+                    row == by_rows - 1, fx[by_rows + 1 : by_rows + 2] * corner[e, 2 * side + 1, f], 0.0
+                )
+                field[k + 1, f, (1, bx + 2)[side]] = total
+                total = own_y[e, side, f] + fy[0:bx] * y_send[e, side, f]
+                total = total + jnp.where(row_x == 0, fy[bx : bx + 1] * corner[e, side, f], 0.0)
+                total = total + jnp.where(row_x == bx - 1, fy[bx + 1 : bx + 2] * corner[e, 2 + side, f], 0.0)
+                y_halo[k + 1, side, f] = total
 
     def within(k):
         for x in range(bx):
@@ -310,6 +332,12 @@
                 if x < bx - 1:
                     total = total + c[0] * field[k, f, x + 3]
                 inner[f, x] = total
+                part_here = total * coef[6, x + 1]
+                for side in range(2):
+                    if x == edge_x[side]:
+                        own_x_send[k // 2, side, f] = part_here
+                    at = edge_y[side]
+                    own_y_send[k // 2, side, f, x : x + 1, :] = part_here[at : at + 1]
 
     def completed(k, f, x):
         total = inner[f, x]
@@ -317,7 +345,7 @@
             total = total + coef[1, 1] * field[k, f, 1]
         if x == bx - 1:
             total = total + coef[0, bx] * field[k, f, bx + 2]
-        low, high = [y_halo[k, side, f, 0, x : x + 1, :] for side in range(2)]
+        low, high = [y_halo[k, side, f, x : x + 1, :] for side in range(2)]
         total = total + jnp.where(row == 0, coef[3, x + 1] * low, 0.0)
         total = total + jnp.where(row == by_rows - 1, coef[2, x + 1] * high, 0.0)
         return field[k, f, x + 2], total
@@ -326,10 +354,10 @@
         if k % 2 == 0:
             send(k)
             if k == 0:
-                start(coef_copies()[0::2])
-                lax.fori_loop(0, bx, stage, 0, unroll=UNROLL)
-                start(coef_copies()[1::2])
+                factors()
+                start(factor_copies())
             within(k)
+            start(own_copies(k))
             arrive(halos(k))
         sums = [nought] * (4 if k + 1 < ITERS else 2)
         for x in range(bx):
@@ -338,7 +366,7 @@
                 if k % 2 == 0:
                     here, total = completed(k, f, x)
                 else:
-                    low, high = [y_halo[k, side, f, 0, x : x + 1, :] for side in range(2)]
+                    low, high = [y_halo[k, side, f, x : x + 1, :] for side in range(2)]
                     here, total = beside(k, f, x, low, high)
                 sums[at] = sums[at] + fold(here * total)
                 at += 1
@@ -353,7 +381,8 @@
             moments += [(sums[0], sums[1])]
         if k % 2 == 0:
             if k == 0:
-                arrive(coef_copies())
+                arrive(factor_copies())
+            arrive(own_copies(k))
             ghosts(k)
 
     rows = 2 * MOMENTS
@@ -386,9 +415,9 @@
 
     lax.fori_loop(0, bx + 1, combine, 0, unroll=bx + 1)
     for f in range(2):
-        rim = weights[f][0] * y_halo[0, 1, f, 0]
+        rim = weights[f][0] * y_halo[0, 1, f]
         for k in range(1, ITERS):
-            rim = rim + weights[f][k] * y_halo[k, 1, f, 0]
+            rim = rim + weights[f][k] * y_halo[k, 1, f]
         rims[f] = rim
     stores = [
         pltpu.make_async_copy(answer, answer_out, out_sem.at[0]),
@@ -398,7 +427,7 @@
         store.start()
     pl.when(has_x[1])(rim_copy_x.wait_send)
     pl.when(has_y[1])(rim_copy_y.wait_send)
-    for sends, _, copy in coef_copies() + halos(0) + halos(2):
+    for sends, _, copy in factor_copies() + own_copies(0) + own_copies(2) + halos(0) + halos(2):
         pl.when(sends)(copy.wait_send)
     pltpu.make_async_copy(others, others, part_send).wait()
     for store in stores:
@@ -462,10 +491,14 @@
         scratch_shapes=[
             vmem((3,) + block, i32), vmem((2, bx, by), i32), vmem(block, f32), vmem((2,) + block, f32), dma((5,)),
             vmem((bx + 1, by, nz), f32), vmem((7, bx + 2, by, nz), f32),
-            vmem((2, 7, bx, nz), f32), vmem((2, 7, bx, nz), f32), dma((4,)), dma((4,)),
+            vmem((2, by + 8, nz), f32), vmem((2, by + 8, nz), f32),
+            vmem((2, bx + 8, nz), f32), vmem((2, bx + 8, nz), f32), dma((4,)), dma((4,)),
+            vmem((ITERS // 2, 2, 2, by, nz), f32), vmem((ITERS // 2, 2, 2, by, nz), f32),
+            vmem((ITERS // 2, 2, 2, bx, nz), f32), vmem((ITERS // 2, 2, 2, bx, nz), f32),
+            dma((ITERS // 2, 4)), dma((ITERS // 2, 4)),
             vmem((by, nz), i32), vmem((bx, 1, nz), i32), vmem((bx, 1, nz), i32), dma((2,)), dma((2,)),
             vmem((ITERS, 2, bx + 4, by, nz), f32),
-            vmem((ITERS // 2, 2, 2, 2, bx, nz), f32), vmem((ITERS, 2, 2, 2, bx, nz), f32),
+            vmem((ITERS // 2, 2, 2, bx, nz), f32), vmem((ITERS, 2, 2, bx, nz), f32),
             vmem((ITERS // 2, 4, 2, 1, nz), f32), vmem((ITERS // 2, 4, 2, 1, nz), f32),
             dma((ITERS // 2, 8)), dma((ITERS // 2, 8)),
             vmem((2,) + block, f32), vmem((1, nz), f32), vmem((nx * ny, 1, nz), f32), dma, dma,

time: 26.9 us -> 25.4 us (0.944)
  Pallas kernels: 26.1 us -> 24.6 us
    pallas_call x1, Pallas kernels: 24.2 us -> 22.7 us  [body(): pl.pallas_call(functools.partial(kernel, nx, ny), out_shape=(jax.ShapeDty...]
where the time goes in v8:
time: 25.4 us; the launch traced here: 25.3 us
  Pallas kernels  24.6 us (97%)
  between operations  0.64 us (3%)
    pallas_call x1, Pallas kernels, body(): pl.pallas_call(functools.partial(kernel, nx, ny), out_shape=(jax.ShapeDty...  22.7 us
    pallas_call x1, Pallas kernels, body(): pl.pallas_call(functools.partial(finish, nx, ny), out_shape=(jax.ShapeDty...  1.88 us

profile of v8, /device:TPU:0, one launch (start us, length us, event | category | flops | bytes accessed | tf_op | source)
XLA Modules:
  0.0 25.3 jit_solution(14460164761670799257)
XLA Ops:
  0.6 22.7 %shard_map.85 = (f32[2,17,16,128]{3,2,1,0:T(8,128)}, f32[2,16,128]{2,1,0:T(8,128)}) custom-call(f32[2,3]{1,0:T(2,128)} %levels.1, s32[3,16,16,128]{3,2,1,0:T(8,128)} %mask_in.1, s32[2,16,16]{2,1,0:T(8,128)} %elec_in.1, f32[16,16,128]{2,1,0:T(8,128)} %leak_in.1, f32[16,16,128]{2,1,0:T(8,128)} %src_in.1, f32[16,16,128]{2,1,0:T(8,128)} %wgt_in.1), custom_call_target="tpu_custom_call" | custom-call | tf_op jit(solution)/shard_map/pallas_call | solution.py:483
  23.4 1.9 %shard_map.86 = (f32[16,16,128]{2,1,0:T(8,128)}, f32[16,16,128]{2,1,0:T(8,128)}, f32[3,16,16,128]{3,2,1,0:T(8,128)}) custom-call(f32[2,17,16,128]{3,2,1,0:T(8,128)} %get-tuple-element.5.answer_in, f32[2,16,128]{2,1,0:T(8,128)} %get-tuple-element.6.rims_in), custom_call_target="tpu_custom_call" | custom-call | tf_op jit(solution)/shard_map/pallas_call | solution.py:511

commit v9 on v8

--- a/solution.py
+++ b/solution.py
@@ -9,6 +9,7 @@
 
 ITERS = 4
 MOMENTS = 2 * ITERS
+EARLY = 5
 MESH = pl.DeviceIdType.MESH
 UNROLL = 4
 VMEM_LIMIT = 62 * 1024 * 1024
@@ -22,14 +23,16 @@
 
     def quadratic(c, m):
         return tree([
-            tree([c[i] * c[k - i] for i in range(max(0, k - len(c) + 1), min(k + 1, len(c)))]) * m[k]
+            tree([c[i] * c[k - i] for i in range(max(0, k - len(c) + 1), min(k + 1, len(c)))]) * m(k)
             for k in range(2 * len(c) - 1)
         ])
 
-    slope = [a - b for a, b in zip(mu[:-1], mu[1:])]
-    one = jnp.ones_like(mu[0])
+    def slope(k):
+        return mu(k) - mu(k + 1)
+
+    one = jnp.ones_like(mu(0))
     scaled, direction, answer = [one], [one], []
-    norm_now = mu[0]
+    norm_now = mu(0)
     for step in range(ITERS):
         alpha = norm_now / quadratic(direction, slope)
         answer = [a + alpha * d for a, d in zip(answer, direction)] + [alpha * direction[-1]]
@@ -350,6 +353,31 @@
         total = total + jnp.where(row == by_rows - 1, coef[2, x + 1] * high, 0.0)
         return field[k, f, x + 2], total
 
+    def picked(rows):
+        return lax.broadcasted_iota(jnp.int32, (rows, nz), 0) == lax.broadcasted_iota(jnp.int32, (rows, nz), 1)
+
+    def share(which, pairs):
+        lines = [jnp.sum(value, axis=0, keepdims=True) for pair in pairs for value in pair]
+        each = jnp.sum(jnp.concatenate(lines, axis=0), axis=1, keepdims=True)
+        message = jnp.sum(jnp.where(picked(len(lines)), each, 0.0), axis=0, keepdims=True)
+        part[which] = message
+        gathered[which, rank] = message
+        each_other(lambda to: pltpu.make_async_remote_copy(
+            part.at[which], gathered.at[which, rank], part_send.at[which], part_recv.at[which],
+            device_id=to, device_id_type=MESH,
+        ).start())
+
+    def bytes_of_others(which, sem):
+        others = gathered.at[which, pl.ds(0, devices - 1)]
+        return pltpu.make_async_copy(others, others, sem.at[which])
+
+    def collect(which, count):
+        bytes_of_others(which, part_recv).wait()
+        message = jnp.sum(gathered[which], axis=0)
+        square = jnp.sum(jnp.where(picked(2 * count), message, 0.0), axis=1, keepdims=True)
+        square = jnp.broadcast_to(square, (2 * count, nz))
+        return [square[2 * k : 2 * k + 2] for k in range(count)]
+
     for k in range(ITERS):
         if k % 2 == 0:
             send(k)
@@ -358,6 +386,8 @@
                 start(factor_copies())
             within(k)
             start(own_copies(k))
+            if len(moments) == EARLY:
+                share(0, moments)
             arrive(halos(k))
         sums = [nought] * (4 if k + 1 < ITERS else 2)
         for x in range(bx):
@@ -385,24 +415,15 @@
             arrive(own_copies(k))
             ghosts(k)
 
-    rows = 2 * MOMENTS
-    pick = lax.broadcasted_iota(jnp.int32, (rows, nz), 0) == lax.broadcasted_iota(jnp.int32, (rows, nz), 1)
-    lines = [jnp.sum(value, axis=0, keepdims=True) for pair in moments for value in pair]
-    each = jnp.sum(jnp.concatenate(lines, axis=0), axis=1, keepdims=True)
-    message = jnp.sum(jnp.where(pick, each, 0.0), axis=0, keepdims=True)
-
-    part[...] = message
-    gathered[rank] = message
-    each_other(lambda to: pltpu.make_async_remote_copy(
-        part, gathered.at[rank], part_send, part_recv, device_id=to, device_id_type=MESH,
-    ).start())
-    others = gathered.at[pl.ds(0, devices - 1)]
-    pltpu.make_async_copy(others, others, part_recv).wait()
-    message = jnp.sum(gathered[...], axis=0)
-
-    square = jnp.sum(jnp.where(pick, message, 0.0), axis=1, keepdims=True)
-    square = jnp.broadcast_to(square, (rows, nz))
-    weights = coefficients([square[2 * k : 2 * k + 2] for k in range(MOMENTS)])
+    share(1, moments[EARLY:])
+    known = list(collect(0, EARLY))
+
+    def moment(k):
+        if k >= len(known):
+            known.extend(collect(1, MOMENTS - EARLY))
+        return known[k]
+
+    weights = coefficients(moment)
     weights = [[jnp.broadcast_to(w[f : f + 1], (by_rows, nz)) for w in weights] for f in range(2)]
 
     def combine(x, carry):
@@ -429,7 +450,8 @@
     pl.when(has_y[1])(rim_copy_y.wait_send)
     for sends, _, copy in factor_copies() + own_copies(0) + own_copies(2) + halos(0) + halos(2):
         pl.when(sends)(copy.wait_send)
-    pltpu.make_async_copy(others, others, part_send).wait()
+    for which in range(2):
+        bytes_of_others(which, part_send).wait()
     for store in stores:
         store.wait()
 
@@ -501,7 +523,7 @@
             vmem((ITERS // 2, 2, 2, bx, nz), f32), vmem((ITERS, 2, 2, bx, nz), f32),
             vmem((ITERS // 2, 4, 2, 1, nz), f32), vmem((ITERS // 2, 4, 2, 1, nz), f32),
             dma((ITERS // 2, 8)), dma((ITERS // 2, 8)),
-            vmem((2,) + block, f32), vmem((1, nz), f32), vmem((nx * ny, 1, nz), f32), dma, dma,
+            vmem((2,) + block, f32), vmem((2, 1, nz), f32), vmem((2, nx * ny, 1, nz), f32), dma((2,)), dma((2,)),
             vmem((2, bx + 1, by, nz), f32), vmem((2, bx, nz), f32), dma((2,)),
         ],
         compiler_params=pltpu.CompilerParams(

time: 25.4 us -> 25.4 us (level)
  no operation moved by 1% of the time
where the time goes in v9:
time: 25.4 us; the launch traced here: 25.2 us
  Pallas kernels  24.6 us (97%)
  between operations  0.64 us (3%)
    pallas_call x1, Pallas kernels, body(): pl.pallas_call(functools.partial(kernel, nx, ny), out_shape=(jax.ShapeDty...  22.7 us
    pallas_call x1, Pallas kernels, body(): pl.pallas_call(functools.partial(finish, nx, ny), out_shape=(jax.ShapeDty...  1.88 us

profile of v9, /device:TPU:0, one launch (start us, length us, event | category | flops | bytes accessed | tf_op | source)
XLA Modules:
  0.0 25.2 jit_solution(18380826934571264059)
XLA Ops:
  0.6 22.7 %shard_map.85 = (f32[2,17,16,128]{3,2,1,0:T(8,128)}, f32[2,16,128]{2,1,0:T(8,128)}) custom-call(f32[2,3]{1,0:T(2,128)} %levels.1, s32[3,16,16,128]{3,2,1,0:T(8,128)} %mask_in.1, s32[2,16,16]{2,1,0:T(8,128)} %elec_in.1, f32[16,16,128]{2,1,0:T(8,128)} %leak_in.1, f32[16,16,128]{2,1,0:T(8,128)} %src_in.1, f32[16,16,128]{2,1,0:T(8,128)} %wgt_in.1), custom_call_target="tpu_custom_call" | custom-call | tf_op jit(solution)/shard_map/pallas_call | solution.py:505
  23.3 1.9 %shard_map.86 = (f32[16,16,128]{2,1,0:T(8,128)}, f32[16,16,128]{2,1,0:T(8,128)}, f32[3,16,16,128]{3,2,1,0:T(8,128)}) custom-call(f32[2,17,16,128]{3,2,1,0:T(8,128)} %get-tuple-element.5.answer_in, f32[2,16,128]{2,1,0:T(8,128)} %get-tuple-element.6.rims_in), custom_call_target="tpu_custom_call" | custom-call | tf_op jit(solution)/shard_map/pallas_call | solution.py:533

commit v10 on v9

--- a/solution.py
+++ b/solution.py
@@ -182,7 +182,7 @@
         leak[x] = leak[x] + first + last + here + here_y + here_z + back_z
         return carry
 
-    lax.fori_loop(0, bx, set_up, 0, unroll=UNROLL)
+    lax.fori_loop(0, bx, set_up, 0, unroll=bx)
     pl.when(has_x[0])(rim_copy_x.wait_recv)
     pl.when(has_y[0])(rim_copy_y.wait_recv)
     cx[0] = conductance(rim_x[...], 0) * x_low
@@ -426,26 +426,21 @@
     weights = coefficients(moment)
     weights = [[jnp.broadcast_to(w[f : f + 1], (by_rows, nz)) for w in weights] for f in range(2)]
 
-    def combine(x, carry):
-        for f in range(2):
-            total = weights[f][0] * field[0, f, x + 2]
-            for k in range(1, ITERS):
-                total = total + weights[f][k] * field[k, f, x + 2]
-            answer[f, x] = total
-        return carry
-
-    lax.fori_loop(0, bx + 1, combine, 0, unroll=bx + 1)
+    stores = [pltpu.make_async_copy(answer.at[f], answer_out.at[f], out_sem.at[f]) for f in range(2)]
+    stores.append(pltpu.make_async_copy(rims, rims_out, out_sem.at[2]))
     for f in range(2):
         rim = weights[f][0] * y_halo[0, 1, f]
         for k in range(1, ITERS):
             rim = rim + weights[f][k] * y_halo[k, 1, f]
         rims[f] = rim
-    stores = [
-        pltpu.make_async_copy(answer, answer_out, out_sem.at[0]),
-        pltpu.make_async_copy(rims, rims_out, out_sem.at[1]),
-    ]
-    for store in stores:
-        store.start()
+    stores[2].start()
+    for f in range(2):
+        for x in range(bx + 1):
+            total = weights[f][0] * field[0, f, x + 2]
+            for k in range(1, ITERS):
+                total = total + weights[f][k] * field[k, f, x + 2]
+            answer[f, x] = total
+        stores[f].start()
     pl.when(has_x[1])(rim_copy_x.wait_send)
     pl.when(has_y[1])(rim_copy_y.wait_send)
     for sends, _, copy in factor_copies() + own_copies(0) + own_copies(2) + halos(0) + halos(2):
@@ -459,20 +454,24 @@
 def finish(nx, ny, answer_in, rims_in, pot_out, adj_out, sens_out, answer, rims, sens, in_sem, out_sem):
     bx, by_rows, nz = pot_out.shape
     loads = [
-        pltpu.make_async_copy(answer_in, answer, in_sem.at[0]),
-        pltpu.make_async_copy(rims_in, rims, in_sem.at[1]),
+        pltpu.make_async_copy(answer_in.at[0], answer.at[0], in_sem.at[0]),
+        pltpu.make_async_copy(answer_in.at[1], answer.at[1], in_sem.at[1]),
+        pltpu.make_async_copy(rims_in, rims, in_sem.at[2]),
     ]
     for load in loads:
         load.start()
     stores = [
         pltpu.make_async_copy(answer.at[0, pl.ds(0, bx)], pot_out, out_sem.at[0]),
         pltpu.make_async_copy(answer.at[1, pl.ds(0, bx)], adj_out, out_sem.at[1]),
-        pltpu.make_async_copy(sens, sens_out, out_sem.at[2]),
     ]
-    loads[0].wait()
-    stores[0].start()
-    stores[1].start()
-    loads[1].wait()
+    half = bx // 2
+    for at in range(2):
+        planes = pl.ds(at * half, half if at == 0 else bx - half)
+        stores.append(pltpu.make_async_copy(sens.at[:, planes], sens_out.at[:, planes], out_sem.at[2 + at]))
+    for f in range(2):
+        loads[f].wait()
+        stores[f].start()
+    loads[2].wait()
     row = lax.broadcasted_iota(jnp.int32, (by_rows, nz), 0)
     lane = lax.broadcasted_iota(jnp.int32, (by_rows, nz), 1)
     x_high = (lax.axis_index("gx") < nx - 1).astype(jnp.float32)
@@ -490,8 +489,11 @@
         sens[2, x] = jnp.where(lane < nz - 1, -gaps[1][2] * gaps[0][2], 0.0)
         return carry
 
-    lax.fori_loop(0, bx, differences, 0, unroll=bx)
-    stores[2].start()
+    for x in range(bx):
+        differences(x, 0)
+        if x == half - 1:
+            stores[2].start()
+    stores[3].start()
     for store in stores:
         store.wait()
 
@@ -524,7 +526,7 @@
             vmem((ITERS // 2, 4, 2, 1, nz), f32), vmem((ITERS // 2, 4, 2, 1, nz), f32),
             dma((ITERS // 2, 8)), dma((ITERS // 2, 8)),
             vmem((2,) + block, f32), vmem((2, 1, nz), f32), vmem((2, nx * ny, 1, nz), f32), dma((2,)), dma((2,)),
-            vmem((2, bx + 1, by, nz), f32), vmem((2, bx, nz), f32), dma((2,)),
+            vmem((2, bx + 1, by, nz), f32), vmem((2, bx, nz), f32), dma((3,)),
         ],
         compiler_params=pltpu.CompilerParams(
             collective_id=0, has_side_effects=True, vmem_limit_bytes=VMEM_LIMIT
@@ -540,7 +542,7 @@
         in_specs=[hbm] * 2,
         out_specs=[hbm] * 3,
         scratch_shapes=[
-            vmem((2, bx + 1, by, nz), f32), vmem((2, bx, nz), f32), vmem((3,) + block, f32), dma((2,)), dma((3,)),
+            vmem((2, bx + 1, by, nz), f32), vmem((2, bx, nz), f32), vmem((3,) + block, f32), dma((3,)), dma((4,)),
         ],
         compiler_params=pltpu.CompilerParams(vmem_limit_bytes=VMEM_LIMIT),
     )(answer, rims)

time: 25.4 us -> 25.4 us (level)
  no operation moved by 1% of the time
where the time goes in v10:
time: 25.4 us; the launch traced here: 25.2 us
  Pallas kernels  24.6 us (97%)
  between operations  0.64 us (3%)
    pallas_call x1, Pallas kernels, body(): pl.pallas_call(functools.partial(kernel, nx, ny), out_shape=(jax.ShapeDty...  22.7 us
    pallas_call x1, Pallas kernels, body(): pl.pallas_call(functools.partial(finish, nx, ny), out_shape=(jax.ShapeDty...  1.88 us

profile of v10, /device:TPU:0, one launch (start us, length us, event | category | flops | bytes accessed | tf_op | source)
XLA Modules:
  0.0 25.2 jit_solution(15740767479472661373)
XLA Ops:
  0.6 22.7 %shard_map.85 = (f32[2,17,16,128]{3,2,1,0:T(8,128)}, f32[2,16,128]{2,1,0:T(8,128)}) custom-call(f32[2,3]{1,0:T(2,128)} %levels.1, s32[3,16,16,128]{3,2,1,0:T(8,128)} %mask_in.1, s32[2,16,16]{2,1,0:T(8,128)} %elec_in.1, f32[16,16,128]{2,1,0:T(8,128)} %leak_in.1, f32[16,16,128]{2,1,0:T(8,128)} %src_in.1, f32[16,16,128]{2,1,0:T(8,128)} %wgt_in.1), custom_call_target="tpu_custom_call" | custom-call | tf_op jit(solution)/shard_map/pallas_call | solution.py:507
  23.3 1.9 %shard_map.86 = (f32[16,16,128]{2,1,0:T(8,128)}, f32[16,16,128]{2,1,0:T(8,128)}, f32[3,16,16,128]{3,2,1,0:T(8,128)}) custom-call(f32[2,17,16,128]{3,2,1,0:T(8,128)} %get-tuple-element.5.answer_in, f32[2,16,128]{2,1,0:T(8,128)} %get-tuple-element.6.rims_in), custom_call_target="tpu_custom_call" | custom-call | tf_op jit(solution)/shard_map/pallas_call | solution.py:535
